TPU v7x, 256 devices: a whole 4x4x8 slice. The times are simulated.
256 devices in a mesh: seq: 32 (over y, z), blk: 8 (over x, core).
Axes of the slice: x: 4, y: 4, z: 8, core: 2. Of those that a mesh axis runs over, the one named last changes fastest.
Arguments:
- teacher_query: bfloat16 [8, 1024, 4096], P('blk', 'seq'), may hold values from -6 to 6
- teacher_key: bfloat16 [8, 1024, 4096], P('blk', 'seq'), may hold values from -6 to 6
- teacher_value: bfloat16 [8, 1024, 4096], P('blk', 'seq'), may hold values from -6 to 6
- student_query: bfloat16 [8, 1024, 4096], P('blk', 'seq'), may hold values from -6 to 6
- student_key: bfloat16 [8, 1024, 4096], P('blk', 'seq'), may hold values from -6 to 6
- student_value: bfloat16 [8, 1024, 4096], P('blk', 'seq'), may hold values from -6 to 6
- frame_index: int32 [8, 1024], P('blk', 'seq'), may hold values from 0 to 6, as said below
Outputs:
- query_grad: bfloat16 [8, 1024, 4096], P('blk', 'seq')
- key_grad: bfloat16 [8, 1024, 4096], P('blk', 'seq')
- value_grad: bfloat16 [8, 1024, 4096], P('blk', 'seq')
Inputs may be any that keep to these rules, and one draw needn't show every extreme that they name: `frame_index`: read row after row, frame numbers never fall; every frame 0 to 6 holds at least (6144) // 6 - 6144 // 24 tokens and at most 2048, and one frame holds exactly 2048.
All inputs are finite; a program needn't handle non-finite values.
Results may differ from a plain program's by a relative error of at most 0.028.
Values may be sent and summed in bfloat16 or wider, within the bound.
No kernel may reach another device: no remote copies, remote signals or barrier semaphores. Data moves between devices by JAX's collectives and lax.ppermute only.
A program may use at most 64 MiB of HBM per device.

v0:
```python
import functools

import jax
import jax.numpy as jnp
from jax import lax
from jax.experimental import pallas as pl
from jax.experimental.pallas import tpu as pltpu
from jax.sharding import PartitionSpec as P

DH = 128
HEADS = 32
SHARD = 32
ROWS = 1024
HALF = 512
TOKENS = 8192
EXTRA = 16
MEMBERS = 32
HALF_MEMBERS = 16
scale = DH ** -0.5
scale_log2 = scale * 1.4426950408889634
loss_scale = 64.0
hidden_bias = -131072.0
f32 = jnp.float32
bf16 = jnp.bfloat16
VMEM = pl.BlockSpec(memory_space=pltpu.VMEM)
SMEM = pl.BlockSpec(memory_space=pltpu.SMEM)
ANY = pl.BlockSpec(memory_space=pl.ANY)


def params():
    return pltpu.CompilerParams(vmem_limit_bytes=60 * 2**20)


def dot(a, b):
    return jnp.dot(a, b, preferred_element_type=f32)


def pack_kernel(count, *refs):
    out_ref = refs[-1]
    for h in range(HEADS):
        for n in range(count):
            out_ref[h, n * SHARD:(n + 1) * SHARD, :] = refs[n][:, h * DH:(h + 1) * DH]
        if len(refs) > count + 1:
            out_ref[h, count * SHARD:, :] = refs[count][...]


def pack(arrays, extra=()):
    count = len(arrays)
    rows = count * SHARD + sum(x.shape[0] for x in extra)
    return pl.pallas_call(
        functools.partial(pack_kernel, count),
        out_shape=jax.ShapeDtypeStruct((HEADS, rows, DH), bf16),
        in_specs=[VMEM] * (count + len(extra)),
        out_specs=VMEM,
        compiler_params=params(),
    )(*arrays, *extra)


def unpack_kernel(in_ref, *out_refs):
    for h in range(HEADS):
        for n in range(len(out_refs)):
            out_refs[n][:, h * DH:(h + 1) * DH] = in_ref[h, n * SHARD:(n + 1) * SHARD, :]


def unpack(rows):
    return pl.pallas_call(
        unpack_kernel,
        out_shape=[jax.ShapeDtypeStruct((SHARD, HEADS * DH), bf16)] * (rows.shape[1] // SHARD),
        in_specs=[VMEM],
        out_specs=[VMEM] * (rows.shape[1] // SHARD),
        compiler_params=params(),
    )(rows)


def fold(op, x):
    return op(x.reshape(-1, 8, x.shape[-1]), axis=0)


def online_step(scores, values_t, cols, max_ref, sum_ref, out_ref):
    before = max_ref[0:1, cols]
    highest = jnp.max(fold(jnp.max, scores), axis=0, keepdims=True) * scale_log2
    now = jnp.maximum(before, highest)
    shrink = jnp.exp2(before - now)
    weights = jnp.exp2(scores * scale_log2 - now)
    rounded = weights.astype(bf16)
    block_sum = jnp.sum(fold(jnp.sum, weights), axis=0, keepdims=True)
    sum_ref[0:1, cols] = sum_ref[0:1, cols] * shrink + block_sum
    out_ref[:, cols] = out_ref[:, cols] * shrink + dot(values_t, rounded)
    max_ref[0:1, cols] = now
    return rounded, now


STATE = [(8, ROWS), (8, ROWS), (DH, ROWS)]


def state_shapes():
    return [jax.ShapeDtypeStruct(shape, f32) for shape in STATE]


def open_state(before, after):
    if before:
        for old, new in zip(before, after):
            new[...] = old[...]
    else:
        after[0][...] = jnp.full((8, ROWS), -1e30, f32)
        after[1][...] = jnp.zeros((8, ROWS), f32)
        after[2][...] = jnp.zeros((DH, ROWS), f32)


def members_of(pieces):
    return sum(piece.shape[0] for piece in pieces)


def load_pieces(pieces, held, sems):
    copies, at = [], 0
    for i, piece in enumerate(pieces):
        members = piece.shape[0]
        copies.append(pltpu.make_async_copy(piece, held.at[pl.ds(at, members)], sems.at[i]))
        at += members
    for copy in copies:
        copy.start()
    return copies


def take(own_ref, other_ref, part, meta_ref):
    rows = slice(part * SHARD, (part + 1) * SHARD)
    own = own_ref[:, rows, :].reshape(HALF, DH)
    other = other_ref[:, rows, :].reshape(HALF, DH)
    own_first = meta_ref[10] > 0
    return jnp.concatenate(
        [jnp.where(own_first, own, other), jnp.where(own_first, other, own)], axis=0
    )


def keys_of(held, i, count=1):
    members = pl.ds(pl.multiple_of(i * MEMBERS, MEMBERS), count * MEMBERS)
    return held[members, :SHARD, :].reshape(count * ROWS, DH)


def values_of(held, i, count=1):
    members = pl.ds(pl.multiple_of(i * MEMBERS, MEMBERS), count * MEMBERS)
    return held[members, SHARD:, :].reshape(count * ROWS, DH)


def keys_of(held, i, count=1):
    members = pl.ds(pl.multiple_of(i * MEMBERS, MEMBERS), count * MEMBERS)
    return held[members, :SHARD, :].reshape(count * ROWS, DH)


def values_of(held, i, count=1):
    members = pl.ds(pl.multiple_of(i * MEMBERS, MEMBERS), count * MEMBERS)
    return held[members, SHARD:, :].reshape(count * ROWS, DH)


def rows_of(i):
    return pl.ds(pl.multiple_of(i * ROWS, ROWS), ROWS)


def teacher_kernel(n_before, n_pieces, last, meta_ref, own_ref, other_ref, *rest):
    before, pieces = rest[:n_before], rest[n_before:n_before + n_pieces]
    rest = rest[n_before + n_pieces:]
    if last:
        target_ref, held, sems = rest[:3]
        state = rest[3:]
    else:
        state, held, sems = rest[:3], rest[3], rest[4]
    copies = load_pieces(pieces, held, sems)
    open_state(before, state)
    queries_t = take(own_ref, other_ref, 0, meta_ref).T
    for copy in copies:
        copy.wait()

    def step(i, _):
        keys = keys_of(held, 2 * i, 2)
        values_t = values_of(held, 2 * i, 2).T
        for first in (0, HALF):
            cols = slice(first, first + HALF)
            online_step(dot(keys, queries_t[:, cols]), values_t, cols, *state)
        return 0

    lax.fori_loop(0, held.shape[0] // (2 * MEMBERS), step, 0)
    if last:
        target_ref[...] = (state[2][...] / state[1][0:1, :]).astype(bf16)


def teacher(meta, own, other, state, pieces, last=False):
    members = members_of(pieces)
    held = pltpu.VMEM((members, 2 * SHARD, DH), bf16)
    scratch = [held, pltpu.SemaphoreType.DMA((len(pieces),))]
    if last:
        out_shape = [jax.ShapeDtypeStruct((DH, ROWS), bf16)]
        scratch += [pltpu.VMEM(shape, f32) for shape in STATE]
    else:
        out_shape = state_shapes()
    return pl.pallas_call(
        functools.partial(teacher_kernel, len(state), len(pieces), last),
        out_shape=out_shape,
        in_specs=[SMEM, VMEM, VMEM] + [VMEM] * len(state) + [ANY] * len(pieces),
        out_specs=[VMEM] * len(out_shape),
        scratch_shapes=scratch,
        compiler_params=params(),
        cost_estimate=pl.CostEstimate(
            flops=members * 6 * 10**7, bytes_accessed=members * 2**14, transcendentals=0
        ),
    )(meta, own, other, *state, *pieces)


def frames_of(tokens, meta_ref):
    frames = jnp.zeros(tokens.shape, jnp.int32)
    for f in range(6):
        frames = frames + (tokens >= meta_ref[f]).astype(jnp.int32)
    return frames


def groups_seen(meta_ref, last):
    seen = jnp.int32(TOKENS)
    for f in range(6, -1, -1):
        seen = jnp.where(last < meta_ref[f], meta_ref[f], seen)
    return (seen + (ROWS - 1)) // ROWS


def keys_with_frames(keys, group, meta_ref):
    column = lax.broadcasted_iota(jnp.int32, (ROWS, DH), 1)
    tokens = group * ROWS + lax.broadcasted_iota(jnp.int32, (ROWS, DH), 0)
    one_hot = (frames_of(tokens, meta_ref) == column).astype(f32).astype(bf16)
    return jnp.concatenate([keys, one_hot], axis=1)


def by_visibility(meta_ref, group, compute, skip=None):
    seen_early = groups_seen(meta_ref, meta_ref[8] + (HALF - 1))
    seen_late = groups_seen(meta_ref, meta_ref[9] + (HALF - 1))

    @pl.when(group < seen_early)
    def _():
        compute(0)

    @pl.when((group >= seen_early) & (group < seen_late))
    def _():
        compute(HALF)

    if skip is not None:

        @pl.when(group >= seen_late)
        def _():
            skip()


def student_kernel(meta_ref, own_ref, other_ref, target_ref, *rest):
    pieces = rest[:10]
    dq_own_ref, dq_other_ref = rest[10:12]
    outs = rest[12:18]
    held, max_ref, sum_ref, out_ref, weights_ref, max_at, dqt, qt_ref, kv_grad = rest[18:27]
    sems, out_sems = rest[27:]
    copies = load_pieces(pieces, held, sems)
    open_state((), (max_ref, sum_ref, out_ref))
    dqt[...] = jnp.zeros(dqt.shape, f32)
    queries = take(own_ref, other_ref, 1, meta_ref)
    column = lax.broadcasted_iota(jnp.int32, (DH, ROWS), 1)
    row = lax.broadcasted_iota(jnp.int32, (DH, ROWS), 0)
    tokens = jnp.where(column < HALF, meta_ref[8] + column, meta_ref[9] + (column - HALF))
    bias = jnp.where((row > frames_of(tokens, meta_ref)) & (row < 7), hidden_bias, 0.0)
    qt_ref[:DH, :] = queries.T
    qt_ref[DH:, :] = bias.astype(bf16)
    for copy in copies:
        copy.wait()

    def forward(i, _):
        group = meta_ref[16 + i]

        def compute(first):
            rows, cols = rows_of(i), slice(first, ROWS)
            keys = keys_with_frames(keys_of(held, i), group, meta_ref)
            rounded, now = online_step(
                dot(keys, qt_ref[:, cols]), values_of(held, i).T, cols, max_ref, sum_ref, out_ref
            )
            weights_ref[rows, cols] = rounded
            at = pl.ds(pl.multiple_of(i * 8, 8), 8)
            max_at[at, cols] = jnp.broadcast_to(now, (8, ROWS - first))

        by_visibility(meta_ref, group, compute)
        return 0

    lax.fori_loop(0, 8, forward, 0)

    inverse = 1.0 / sum_ref[0:1, :]
    output = out_ref[...] * inverse
    out_grad = (loss_scale * (output - target_ref[...].astype(f32))).astype(bf16).astype(f32)
    delta = jnp.sum(out_grad * output, axis=0, keepdims=True) * inverse
    grad_t = (out_grad * inverse).astype(bf16)
    delta_1 = delta.astype(bf16).astype(f32)
    delta_2 = (delta - delta_1).astype(bf16).astype(f32)
    delta_3 = delta - delta_1 - delta_2
    delta_rows = jnp.where(
        row == 0, -delta_1, jnp.where(row == 1, -delta_2, jnp.where(row == 2, -delta_3, 0.0))
    )
    grad_delta_t = jnp.concatenate([grad_t, delta_rows.astype(bf16)], axis=0)
    grad = grad_t.T
    key_column = lax.broadcasted_iota(jnp.int32, (ROWS, DH), 1)
    ones = jnp.where(key_column < 3, 1.0, 0.0).astype(bf16)

    def backward(i, _):
        group = meta_ref[16 + i]

        def compute(first):
            rows, cols = rows_of(i), slice(first, ROWS)
            values = jnp.concatenate([values_of(held, i), ones], axis=1)
            centred = dot(values, grad_delta_t[:, cols])
            at = pl.ds(pl.multiple_of(i * 8, 8), 8)
            shrink = jnp.exp2(max_at[at, cols][0:1] - max_ref[0:1, cols])
            weights = weights_ref[rows, cols].astype(f32) * shrink
            score_grad = (weights * centred).astype(bf16)
            members = pl.ds(pl.multiple_of(i * MEMBERS, MEMBERS), MEMBERS)
            value_grad = dot(weights.astype(bf16), grad[cols])
            key_grad = dot(score_grad, queries[cols]) * scale
            kv_grad[members, SHARD:, :] = value_grad.astype(bf16).reshape(MEMBERS, SHARD, DH)
            kv_grad[members, :SHARD, :] = key_grad.astype(bf16).reshape(MEMBERS, SHARD, DH)
            dqt[:, cols] += dot(keys_of(held, i).T, score_grad)

        def skip():
            members = pl.ds(pl.multiple_of(i * MEMBERS, MEMBERS), MEMBERS)
            kv_grad[members, :, :] = jnp.zeros((MEMBERS, 2 * SHARD, DH), bf16)

        by_visibility(meta_ref, group, compute, skip)
        return 0

    lax.fori_loop(0, 8, backward, 0)
    out_copies = [
        pltpu.make_async_copy(kv_grad.at[pl.ds(i * MEMBERS, MEMBERS)], out, out_sems.at[k])
        for k, (i, out) in enumerate(
            [(0, outs[0]), (1, outs[1]), (2, outs[2].at[0]), (4, outs[2].at[1])]
            + [(3, outs[3].at[0]), (5, outs[3].at[1]), (6, outs[4]), (7, outs[5])]
        )
    ]
    for copy in out_copies:
        copy.start()
    query_grad = (dqt[...] * scale).T.astype(bf16)
    own_first = meta_ref[10] > 0
    first, second = query_grad[:HALF], query_grad[HALF:]
    shape = (HALF_MEMBERS, SHARD, DH)
    dq_own_ref[...] = jnp.where(own_first, first, second).reshape(shape)
    dq_other_ref[...] = jnp.where(own_first, second, first).reshape(shape)
    for copy in out_copies:
        copy.wait()


def student(meta, own, other, target, pieces):
    half = jax.ShapeDtypeStruct((HALF_MEMBERS, SHARD, DH), bf16)
    one = jax.ShapeDtypeStruct((MEMBERS, 2 * SHARD, DH), bf16)
    two = jax.ShapeDtypeStruct((2, MEMBERS, 2 * SHARD, DH), bf16)
    return pl.pallas_call(
        student_kernel,
        out_shape=[half, half, one, one, two, two, one, one],
        in_specs=[SMEM, VMEM, VMEM, VMEM] + [ANY] * 10,
        out_specs=[VMEM] * 2 + [ANY] * 6,
        scratch_shapes=[
            pltpu.VMEM((8 * MEMBERS, 2 * SHARD, DH), bf16),
            pltpu.VMEM((8, ROWS), f32),
            pltpu.VMEM((8, ROWS), f32),
            pltpu.VMEM((DH, ROWS), f32),
            pltpu.VMEM((TOKENS, ROWS), bf16),
            pltpu.VMEM((64, ROWS), f32),
            pltpu.VMEM((DH, ROWS), f32),
            pltpu.VMEM((2 * DH, ROWS), bf16),
            pltpu.VMEM((8 * MEMBERS, 2 * SHARD, DH), bf16),
            pltpu.SemaphoreType.DMA((10,)),
            pltpu.SemaphoreType.DMA((8,)),
        ],
        compiler_params=params(),
        cost_estimate=pl.CostEstimate(
            flops=26 * 10**9, bytes_accessed=10 * 2**20, transcendentals=ROWS * TOKENS
        ),
    )(meta, own, other, target, *pieces)


def exchange(packed):
    return lax.all_to_all(packed, "seq", split_axis=0, concat_axis=0, tiled=True)


def trade(x):
    return lax.ppermute(x, "blk", [(i, 7 - i) for i in range(8)])


def chip_shift(x, by):
    return lax.ppermute(x, "blk", [(i, ((i // 2 + by) % 4) * 2 + i % 2) for i in range(8)])


def swap_cores(x):
    return lax.ppermute(x, "blk", [(i, i ^ 1) for i in range(8)])


def with_other_core(parts):
    return [x for part in parts for x in (part, swap_cores(part))]


def frame_ends(counted):
    counts = jnp.broadcast_to(jnp.sum(counted.astype(f32), axis=0)[:, None], (8, DH))
    counts = counts + swap_cores(counts)
    counts = counts + chip_shift(counts, 1)
    counts = counts + chip_shift(counts, 2)
    return counts[:, 0].astype(jnp.int32)


def per_device(
    teacher_query,
    teacher_key,
    teacher_value,
    student_query,
    student_key,
    student_value,
    frame_index,
):
    blk = lax.axis_index("blk")
    seq = lax.axis_index("seq")
    frame_ids = jnp.arange(DH, dtype=jnp.int32)
    counts = jnp.sum((frame_index[0][:, None] <= frame_ids[None, :]).astype(f32), axis=0)
    counts = jnp.broadcast_to(counts.astype(bf16), (EXTRA, DH))
    tie = lax.optimization_barrier
    arrays = (teacher_key, teacher_value, teacher_query, student_query)
    moved = exchange(pack([x[0] for x in arrays], (counts,)))
    student_key, student_value, moved = tie((student_key, student_value, moved))
    student_kv = exchange(pack([student_key[0], student_value[0]]))
    teacher_kv = moved[:, :2 * SHARD]
    early = seq < HALF_MEMBERS
    keep = jnp.where(early, 0, HALF_MEMBERS)

    def half_of(x, at):
        return lax.dynamic_slice_in_dim(x, at, HALF_MEMBERS, axis=0)

    queries = moved[:, 2 * SHARD:4 * SHARD]
    own = half_of(queries, keep)
    other = trade(half_of(queries, HALF_MEMBERS - keep))

    chip, core = blk // 2, blk % 2
    own_start = blk * ROWS + jnp.where(early, 0, HALF)
    other_start = (7 - blk) * ROWS + jnp.where(early, HALF, 0)
    halves = jnp.stack([jnp.minimum(own_start, other_start), jnp.maximum(own_start, other_start)])
    groups = []
    for by in (0, 1, 3, 2):
        groups += [((chip + by) % 4) * 2 + core, ((chip + by) % 4) * 2 + 1 - core]
    own_first = (own_start < other_start).astype(jnp.int32)
    place = [halves, own_first[None], jnp.zeros((5,), jnp.int32), jnp.stack(groups)]
    place = jnp.concatenate([jnp.zeros((8,), jnp.int32)] + place).astype(jnp.int32)

    def near_pieces(after, before):
        return with_other_core([after, before])

    def far_halves(before, after):
        return [chip_shift(before[:HALF_MEMBERS], 1), chip_shift(after[HALF_MEMBERS:], 3)]

    teacher_after, teacher_before = chip_shift(teacher_kv, 3), chip_shift(teacher_kv, 1)
    student_after, student_before = chip_shift(student_kv, 3), chip_shift(student_kv, 1)
    ends = frame_ends(moved[:, 4 * SHARD, :8])
    meta = jnp.concatenate([ends, place[8:]])
    teacher_here = with_other_core([teacher_kv])
    teacher_near = near_pieces(teacher_after, teacher_before)
    teacher_far = far_halves(teacher_before, teacher_after)
    teacher_far += [swap_cores(x) for x in teacher_far]
    student_here = with_other_core([student_kv])
    student_near = near_pieces(student_after, student_before)

    (target,) = teacher(
        place, own, other, [], teacher_here + teacher_near + teacher_far, last=True
    )
    student_before, student_after, target = tie((student_before, student_after, target))
    student_halves = far_halves(student_before, student_after)
    student_far = student_halves + [swap_cores(x) for x in student_halves]
    grads = student(meta, own, other, target, student_here + student_near + student_far)
    query_own, query_other, here_mine, here_other, near_mine, near_other, far_mine, far_other = grads
    far = (far_mine.astype(f32) + swap_cores(far_other).astype(f32)).astype(bf16)
    query_back = trade(query_other)
    by_ahead = chip_shift(far[:HALF_MEMBERS], 1).astype(f32)
    by_behind = chip_shift(far[HALF_MEMBERS:], 3).astype(f32)
    near = near_mine.astype(f32) + swap_cores(near_other).astype(f32)
    ahead = jnp.concatenate([near[0, :HALF_MEMBERS] + by_ahead, near[0, HALF_MEMBERS:]])
    behind = jnp.concatenate([near[1, :HALF_MEMBERS], near[1, HALF_MEMBERS:] + by_behind])
    total = here_mine.astype(f32) + swap_cores(here_other).astype(f32)
    for part in (chip_shift(ahead.astype(bf16), 1), chip_shift(behind.astype(bf16), 3)):
        total = total + part.astype(f32)
    query_grad = jnp.concatenate(
        [jnp.where(early, query_own, query_back), jnp.where(early, query_back, query_own)]
    )
    (query_out,) = unpack(exchange(query_grad))
    key_out, value_out = unpack(exchange(total.astype(bf16)))
    return (query_out[None], key_out[None], value_out[None])


def solution(mesh):
    spec = P("blk", "seq", None)
    return jax.shard_map(
        per_device,
        mesh=mesh,
        in_specs=(spec,) * 6 + (P("blk", "seq"),),
        out_specs=(spec,) * 3,
        check_vma=False,
    )
```

profile of v0, /device:TPU:32, one launch (start us, length us, event | category | flops | bytes accessed | tf_op | source)
XLA Modules:
  0.0 210.1 jit_solution(10257914157418439489)
XLA Ops:
  2.0 2.4 %shard_map.94 = bf16[32,144,128]{2,1,0:T(8,128)(2,1)} custom-call(bf16[32,4096]{1,0:T(8,128)(2,1)} %bitcast.39, bf16[32,4096]{1,0:T(8,128)(2,1)} %bitcast.40, bf16[32,4096]{1,0:T(8,128)(2,1)} %bitcast.41, bf16[32,4096]{1,0:T(8,128)(2,1)} %bitcast.42, bf16[16,128]{1,0:T(8,128)(2,1)} %broadcast_in_dim.25.refs_4_), custom_call_target="tpu_custom_call" | custom-call | tf_op jit(solution)/shard_map/pallas_call | solution.py:50
  4.4 43.5 %all_to_all.20 = bf16[32,144,128]{2,1,0:T(8,128)(2,1)S(1)} all-to-all(bf16[32,144,128]{2,1,0:T(8,128)(2,1)} %shard_map.94), channel_id=1, replica_groups=mesh['seq'=32,'blk'=8] {'seq'}, dimensions={0} | all-to-all | bytes 2359296 | tf_op jit(solution)/shard_map/all_to_all | solution.py:376
  48.0 1.6 collective-permute-start.9
  49.6 1.7 collective-permute-start.7
  51.4 1.9 shard_map.95
  53.3 4.6 %all-to-all-start.1 = ((bf16[32,64,128]{2,1,0:T(8,128)(2,1)}), bf16[32,64,128]{2,1,0:T(8,128)(2,1)S(1)}, u32[]{:S(2)}, u32[]{:S(2)}) async-start(bf16[32,64,128]{2,1,0:T(8,128)(2,1)} %shard_map.95), calls=%async_computation.1 | async-start | bytes 1048576 | tf_op jit(solution)/shard_map/all_to_all | solution.py:376
  58.7 1.7 collective-permute-start
  63.4 4.2 %collective-permute-done.1 = f32[8,128]{0,1:T(8,128)S(1)} collective-permute-done((f32[8,128]{0,1:T(8,128)S(1)}, f32[8,128]{0,1:T(8,128)S(1)}, u32[]{:S(2)}, u32[]{:S(2)}) %collective-permute-start.1) | collective-permute-done | bytes 4128 | tf_op jit(solution)/shard_map/ppermute | solution.py:384
  68.5 1.6 collective-permute-start.8
  70.1 3.2 %collective-permute-done.11.rest_6_ = bf16[16,64,128]{2,1,0:T(8,128)(2,1)S(1)} collective-permute-done((bf16[16,64,128]{2,1,0:T(8,128)(2,1)S(1)}, bf16[16,64,128]{2,1,0:T(8,128)(2,1)S(1)}, u32[]{:S(2)}, u32[]{:S(2)}) %collective-permute-start.11) | collective-permute-done | bytes 262176 | tf_op jit(solution)/shard_map/ppermute | solution.py:384
  73.2 1.2 collective-permute-start.13
  75.4 1.3 collective-permute-start.14
  77.3 1.2 collective-permute-start.2
  78.6 1.5 collective-permute-start.5
  80.8 17.2 %shard_map.96.target_ref = bf16[128,1024]{1,0:T(8,128)(2,1)} custom-call(s32[24]{0:T(128)} %concatenate.20.meta_ref, bf16[16,64,128]{2,1,0:T(8,128)(2,1)} %get-tuple-element.46.own_ref, bf16[16,64,128]{2,1,0:T(8,128)(2,1)} %copy-done.13, bf16[32,64,128]{2,1,0:T(8,128)(2,1)} %copy-done.5, bf16[32,64,128]{2,1,0:T(8,128)(2,1)} %copy-done.10, ...), custom_call_target="tpu_custom_call" | custom-call | flops 15360000000 | bytes 4194304 | tf_op jit(solution)/shard_map/pallas_call | solution.py:195
  98.1 2.7 %collective-permute-start.19 = (bf16[16,64,128]{2,1,0:T(8,128)(2,1)S(1)}, bf16[16,64,128]{2,1,0:T(8,128)(2,1)S(1)}, u32[]{:S(2)}, u32[]{:S(2)}) collective-permute-start(bf16[16,64,128]{2,1,0:T(8,128)(2,1)S(1)} %slice.53), channel_id=1, source_target_pairs={{0,6},{1,7},{2,0},{3,1},{4,2},{5,3},{6,4},{7,5},{8,14},{9,15},{10,... | collective-permute-start | bytes 786440 | tf_op jit(solution)/shard_map/ppermute | solution.py:384
  101.3 5.1 %collective-permute-done.19.rest_7_ = bf16[16,64,128]{2,1,0:T(8,128)(2,1)S(1)} collective-permute-done((bf16[16,64,128]{2,1,0:T(8,128)(2,1)S(1)}, bf16[16,64,128]{2,1,0:T(8,128)(2,1)S(1)}, u32[]{:S(2)}, u32[]{:S(2)}) %collective-permute-start.19) | collective-permute-done | bytes 262176 | tf_op jit(solution)/shard_map/ppermute | solution.py:384
  106.4 4.3 %collective-permute-done.18.rest_6_ = bf16[16,64,128]{2,1,0:T(8,128)(2,1)S(1)} collective-permute-done((bf16[16,64,128]{2,1,0:T(8,128)(2,1)S(1)}, bf16[16,64,128]{2,1,0:T(8,128)(2,1)S(1)}, u32[]{:S(2)}, u32[]{:S(2)}) %collective-permute-start.18) | collective-permute-done | bytes 262176 | tf_op jit(solution)/shard_map/ppermute | solution.py:384
  112.4 30.0 %shard_map.97 = (bf16[16,32,128]{2,1,0:T(8,128)(2,1)}, bf16[16,32,128]{2,1,0:T(8,128)(2,1)}, bf16[32,64,128]{2,1,0:T(8,128)(2,1)}, bf16[32,64,128]{2,1,0:T(8,128...) custom-call(s32[24]{0:T(128)} %concatenate.19.meta_ref, ...), custom_call_target="tpu_custom_call" | custom-call | flops 25999998976 | bytes 10485760 | tf_op jit(solution)/shard_map/pallas_call | solution.py:350
  142.5 4.3 %collective-permute-start.24 = (bf16[2,32,64,128]{3,2,1,0:T(8,128)(2,1)}, bf16[2,32,64,128]{3,2,1,0:T(8,128)(2,1)S(1)}, u32[]{:S(2)}, u32[]{:S(2)}) collective-permute-start(bf16[2,32,64,128]{3,2,1,0:T(8,128)(2,1)} %get-tuple-element.30), channel_id=1, source_target_pairs={{0,1},{1,0},{2,3},{3,2},{4,5},{5,4},{6,7},{7,6},{8,9},{9,8},{10,11... | collective-permute-start | bytes 3145736 | tf_op jit(solution)/shard_map/ppermute | solution.py:388
  147.3 2.7 %collective-permute-done.25 = bf16[32,64,128]{2,1,0:T(8,128)(2,1)S(1)} collective-permute-done((bf16[32,64,128]{2,1,0:T(8,128)(2,1)}, bf16[32,64,128]{2,1,0:T(8,128)(2,1)S(1)}, u32[]{:S(2)}, u32[]{:S(2)}) %collective-permute-start.25) | collective-permute-done | bytes 524320 | tf_op jit(solution)/shard_map/ppermute | solution.py:388
  150.0 1.2 add_convert_fusion.1
  151.4 3.2 %collective-permute-start.28 = (bf16[16,64,128]{2,1,0:T(8,128)(2,1)S(1)}, bf16[16,64,128]{2,1,0:T(8,128)(2,1)S(1)}, u32[]{:S(2)}, u32[]{:S(2)}) collective-permute-start(bf16[16,64,128]{2,1,0:T(8,128)(2,1)S(1)} %get-tuple-element.44), channel_id=1, source_target_pairs={{0,6},{1,7},{2,0},{3,1},{4,2},{5,3},{6,4},{7,5},{8,14},{9,15},{10,... | collective-permute-start | bytes 786440 | tf_op jit(solution)/shard_map/ppermute | solution.py:384
  155.1 6.0 %collective-permute-done.26 = bf16[16,64,128]{2,1,0:T(8,128)(2,1)S(1)} collective-permute-done((bf16[16,64,128]{2,1,0:T(8,128)(2,1)S(1)}, bf16[16,64,128]{2,1,0:T(8,128)(2,1)S(1)}, u32[]{:S(2)}, u32[]{:S(2)}) %collective-permute-start.26) | collective-permute-done | bytes 262176 | tf_op jit(solution)/shard_map/ppermute | solution.py:384
  161.4 3.0 %collective-permute-start.29 = (bf16[32,64,128]{2,1,0:T(8,128)(2,1)S(1)}, bf16[32,64,128]{2,1,0:T(8,128)(2,1)S(1)}, u32[]{:S(2)}, u32[]{:S(2)}) collective-permute-start(bf16[32,64,128]{2,1,0:T(8,128)(2,1)S(1)} %pad_maximum_fusion.1), channel_id=1, source_target_pairs={{0,6},{1,7},{2,0},{3,1},{4,2},{5,3},{6,4},{7,5},{8,14},{9,15},{10,... | collective-permute-start | bytes 1572872 | tf_op jit(solution)/shard_map/ppermute | solution.py:384
  165.3 9.9 %all-to-all-start.2 = ((bf16[32,32,128]{2,1,0:T(8,128)(2,1)}), bf16[32,32,128]{2,1,0:T(8,128)(2,1)S(1)}, u32[]{:S(2)}, u32[]{:S(2)}) async-start(bf16[32,32,128]{2,1,0:T(8,128)(2,1)} %pad_maximum_fusion.2), calls=%async_computation.2 | async-start | bytes 524288 | tf_op jit(solution)/shard_map/all_to_all | solution.py:376
  175.2 3.3 %collective-permute-done.27 = bf16[32,64,128]{2,1,0:T(8,128)(2,1)S(1)} collective-permute-done((bf16[32,64,128]{2,1,0:T(8,128)(2,1)S(1)}, bf16[32,64,128]{2,1,0:T(8,128)(2,1)S(1)}, u32[]{:S(2)}, u32[]{:S(2)}) %collective-permute-start.27) | collective-permute-done | bytes 524320 | tf_op jit(solution)/shard_map/ppermute | solution.py:384
  179.7 6.9 %all-to-all-done.2.in_ref = bf16[32,32,128]{2,1,0:T(8,128)(2,1)S(1)} async-done(((bf16[32,32,128]{2,1,0:T(8,128)(2,1)}), bf16[32,32,128]{2,1,0:T(8,128)(2,1)S(1)}, u32[]{:S(2)}, u32[]{:S(2)}) %all-to-all-start.2) | async-done | bytes 262176 | tf_op jit(solution)/shard_map/all_to_all | solution.py:376
  186.6 4.6 %all-to-all-start.3 = ((bf16[32,64,128]{2,1,0:T(8,128)(2,1)}), bf16[32,64,128]{2,1,0:T(8,128)(2,1)S(1)}, u32[]{:S(2)}, u32[]{:S(2)}) async-start(bf16[32,64,128]{2,1,0:T(8,128)(2,1)} %add_convert_fusion), calls=%async_computation.3 | async-start | bytes 1048576 | tf_op jit(solution)/shard_map/all_to_all | solution.py:376
  191.2 1.7 shard_map.98
  192.9 14.4 %all-to-all-done.3.in_ref = bf16[32,64,128]{2,1,0:T(8,128)(2,1)S(1)} async-done(((bf16[32,64,128]{2,1,0:T(8,128)(2,1)}), bf16[32,64,128]{2,1,0:T(8,128)(2,1)S(1)}, u32[]{:S(2)}, u32[]{:S(2)}) %all-to-all-start.3) | async-done | bytes 524320 | tf_op jit(solution)/shard_map/all_to_all | solution.py:376
  208.1 1.9 shard_map.99
  (104 shorter events, 14.8 us)
Async XLA Ops:
  48.0 13.8 %collective-permute-start.9 = (bf16[32,64,128]{2,1,0:T(8,128)(2,1)S(1)}, bf16[32,64,128]{2,1,0:T(8,128)(2,1)S(1)}, u32[]{:S(2)}, u32[]{:S(2)}) collective-permute-start(bf16[32,64,128]{2,1,0:T(8,128)(2,1)S(1)} %get-tuple-element.39.rest_0_), channel_id=1, source_target_pairs={{0,2},{1,3},{2,4},{3,5},{4,6},{5,7},{6,0},{7,1},{8,10},{9,11},{10,... | collective-permute-start | bytes 1572872 | tf_op jit(solution)/shard_map/ppermute | solution.py:384
  49.6 12.8 %collective-permute-start.7 = (bf16[32,64,128]{2,1,0:T(8,128)(2,1)S(1)}, bf16[32,64,128]{2,1,0:T(8,128)(2,1)}, u32[]{:S(2)}, u32[]{:S(2)}) collective-permute-start(bf16[32,64,128]{2,1,0:T(8,128)(2,1)S(1)} %get-tuple-element.39.rest_0_), channel_id=1, source_target_pairs={{0,6},{1,7},{2,0},{3,1},{4,2},{5,3},{6,4},{7,5},{8,14},{9,15},{10,... | collective-permute-start | bytes 1572872 | tf_op jit(solution)/shard_map/ppermute | solution.py:384
  53.3 25.2 %all-to-all-start.1 = ((bf16[32,64,128]{2,1,0:T(8,128)(2,1)}), bf16[32,64,128]{2,1,0:T(8,128)(2,1)S(1)}, u32[]{:S(2)}, u32[]{:S(2)}) async-start(bf16[32,64,128]{2,1,0:T(8,128)(2,1)} %shard_map.95), calls=%async_computation.1 | async-start | bytes 1048576 | tf_op jit(solution)/shard_map/all_to_all | solution.py:376
  58.6 9.8 %collective-permute-start.3 = (bf16[16,64,128]{2,1,0:T(8,128)(2,1)S(1)}, bf16[16,64,128]{2,1,0:T(8,128)(2,1)S(1)}, u32[]{:S(2)}, u32[]{:S(2)}) collective-permute-start(bf16[16,64,128]{2,1,0:T(8,128)(2,1)S(1)} %get-tuple-element.45), channel_id=1, source_target_pairs={{0,7},{1,6},{2,5},{3,4},{4,3},{5,2},{6,1},{7,0},{8,15},{9,14},{10,... | collective-permute-start | bytes 786440 | tf_op jit(solution)/shard_map/ppermute | solution.py:380
  58.7 2.6 %collective-permute-start = (f32[8,128]{0,1:T(8,128)S(1)}, f32[8,128]{0,1:T(8,128)S(1)}, u32[]{:S(2)}, u32[]{:S(2)}) collective-permute-start(f32[8,128]{0,1:T(8,128)S(1)} %broadcast_in_dim.26), channel_id=1, source_target_pairs={{0,1},{1,0},{2,3},{3,2},{4,5},{5,4},{6,7},{7,6},{8,9},{9,8},{10,11... | collective-permute-start | bytes 12296 | tf_op jit(solution)/shard_map/ppermute | solution.py:388
  61.4 6.3 %collective-permute-start.1 = (f32[8,128]{0,1:T(8,128)S(1)}, f32[8,128]{0,1:T(8,128)S(1)}, u32[]{:S(2)}, u32[]{:S(2)}) collective-permute-start(f32[8,128]{0,1:T(8,128)S(1)} %broadcast_add_fusion), channel_id=1, source_target_pairs={{0,2},{1,3},{2,4},{3,5},{4,6},{5,7},{6,0},{7,1},{8,10},{9,11},{10,... | collective-permute-start | bytes 12296 | tf_op jit(solution)/shard_map/ppermute | solution.py:384
  61.6 15.7 %collective-permute-start.6 = (bf16[32,64,128]{2,1,0:T(8,128)(2,1)S(1)}, bf16[32,64,128]{2,1,0:T(8,128)(2,1)S(1)}, u32[]{:S(2)}, u32[]{:S(2)}) collective-permute-start(bf16[32,64,128]{2,1,0:T(8,128)(2,1)S(1)} %get-tuple-element.39.rest_0_), channel_id=1, source_target_pairs={{0,1},{1,0},{2,3},{3,2},{4,5},{5,4},{6,7},{7,6},{8,9},{9,8},{10,11... | collective-permute-start | bytes 1572872 | tf_op jit(solution)/shard_map/ppermute | solution.py:388
  61.9 11.3 %collective-permute-start.11 = (bf16[16,64,128]{2,1,0:T(8,128)(2,1)S(1)}, bf16[16,64,128]{2,1,0:T(8,128)(2,1)S(1)}, u32[]{:S(2)}, u32[]{:S(2)}) collective-permute-start(bf16[16,64,128]{2,1,0:T(8,128)(2,1)S(1)} %slice.62), channel_id=1, source_target_pairs={{0,2},{1,3},{2,4},{3,5},{4,6},{5,7},{6,0},{7,1},{8,10},{9,11},{10,... | collective-permute-start | bytes 786440 | tf_op jit(solution)/shard_map/ppermute | solution.py:384
  62.4 16.2 %collective-permute-start.10 = (bf16[32,64,128]{2,1,0:T(8,128)(2,1)S(1)}, bf16[32,64,128]{2,1,0:T(8,128)(2,1)}, u32[]{:S(2)}, u32[]{:S(2)}) collective-permute-start(bf16[32,64,128]{2,1,0:T(8,128)(2,1)S(1)} %collective-permute-done.9.rest_4_), channel_id=1, source_target_pairs={{0,1},{1,0},{2,3},{3,2},{4,5},{5,4},{6,7},{7,6},{8,9},{9,8},{10,11... | collective-permute-start | bytes 1572872 | tf_op jit(solution)/shard_map/ppermute | solution.py:388
  67.6 7.7 %collective-permute-start.12 = (bf16[16,64,128]{2,1,0:T(8,128)(2,1)S(1)}, bf16[16,64,128]{2,1,0:T(8,128)(2,1)S(1)}, u32[]{:S(2)}, u32[]{:S(2)}) collective-permute-start(bf16[16,64,128]{2,1,0:T(8,128)(2,1)S(1)} %slice.63), channel_id=1, source_target_pairs={{0,6},{1,7},{2,0},{3,1},{4,2},{5,3},{6,4},{7,5},{8,14},{9,15},{10,... | collective-permute-start | bytes 786440 | tf_op jit(solution)/shard_map/ppermute | solution.py:384
  68.5 12.3 %collective-permute-start.8 = (bf16[32,64,128]{2,1,0:T(8,128)(2,1)}, bf16[32,64,128]{2,1,0:T(8,128)(2,1)}, u32[]{:S(2)}, u32[]{:S(2)}) collective-permute-start(bf16[32,64,128]{2,1,0:T(8,128)(2,1)} %collective-permute-done.7.rest_2_), channel_id=1, source_target_pairs={{0,1},{1,0},{2,3},{3,2},{4,5},{5,4},{6,7},{7,6},{8,9},{9,8},{10,11... | collective-permute-start | bytes 1572872 | tf_op jit(solution)/shard_map/ppermute | solution.py:388
  73.2 5.3 %collective-permute-start.13 = (bf16[16,64,128]{2,1,0:T(8,128)(2,1)S(1)}, bf16[16,64,128]{2,1,0:T(8,128)(2,1)}, u32[]{:S(2)}, u32[]{:S(2)}) collective-permute-start(bf16[16,64,128]{2,1,0:T(8,128)(2,1)S(1)} %collective-permute-done.11.rest_6_), channel_id=1, source_target_pairs={{0,1},{1,0},{2,3},{3,2},{4,5},{5,4},{6,7},{7,6},{8,9},{9,8},{10,11... | collective-permute-start | bytes 786440 | tf_op jit(solution)/shard_map/ppermute | solution.py:388
  75.4 4.8 %collective-permute-start.14 = (bf16[16,64,128]{2,1,0:T(8,128)(2,1)S(1)}, bf16[16,64,128]{2,1,0:T(8,128)(2,1)}, u32[]{:S(2)}, u32[]{:S(2)}) collective-permute-start(bf16[16,64,128]{2,1,0:T(8,128)(2,1)S(1)} %collective-permute-done.12.rest_7_), channel_id=1, source_target_pairs={{0,1},{1,0},{2,3},{3,2},{4,5},{5,4},{6,7},{7,6},{8,9},{9,8},{10,11... | collective-permute-start | bytes 786440 | tf_op jit(solution)/shard_map/ppermute | solution.py:388
  77.3 24.0 %collective-permute-start.2 = (f32[8,128]{0,1:T(8,128)S(1)}, f32[8,128]{0,1:T(8,128)S(1)}, u32[]{:S(2)}, u32[]{:S(2)}) collective-permute-start(f32[8,128]{0,1:T(8,128)S(1)} %fusion.9), channel_id=1, source_target_pairs={{0,4},{1,5},{2,6},{3,7},{4,0},{5,1},{6,2},{7,3},{8,12},{9,13},{10,... | collective-permute-start | bytes 12296 | tf_op jit(solution)/shard_map/ppermute | solution.py:384
  78.5 32.8 %collective-permute-start.15 = (bf16[32,64,128]{2,1,0:T(8,128)(2,1)S(1)}, bf16[32,64,128]{2,1,0:T(8,128)(2,1)}, u32[]{:S(2)}, u32[]{:S(2)}) collective-permute-start(bf16[32,64,128]{2,1,0:T(8,128)(2,1)S(1)} %all-to-all-done.1.rest_0_), channel_id=1, source_target_pairs={{0,1},{1,0},{2,3},{3,2},{4,5},{5,4},{6,7},{7,6},{8,9},{9,8},{10,11... | collective-permute-start | bytes 1572872 | tf_op jit(solution)/shard_map/ppermute | solution.py:388
  78.6 19.4 %collective-permute-start.5 = (bf16[32,64,128]{2,1,0:T(8,128)(2,1)S(1)}, bf16[32,64,128]{2,1,0:T(8,128)(2,1)S(1)}, u32[]{:S(2)}, u32[]{:S(2)}) collective-permute-start(bf16[32,64,128]{2,1,0:T(8,128)(2,1)S(1)} %all-to-all-done.1.rest_0_), channel_id=1, source_target_pairs={{0,6},{1,7},{2,0},{3,1},{4,2},{5,3},{6,4},{7,5},{8,14},{9,15},{10,... | collective-permute-start | bytes 1572872 | tf_op jit(solution)/shard_map/ppermute | solution.py:384
  80.1 17.9 %collective-permute-start.4 = (bf16[32,64,128]{2,1,0:T(8,128)(2,1)S(1)}, bf16[32,64,128]{2,1,0:T(8,128)(2,1)S(1)}, u32[]{:S(2)}, u32[]{:S(2)}) collective-permute-start(bf16[32,64,128]{2,1,0:T(8,128)(2,1)S(1)} %all-to-all-done.1.rest_0_), channel_id=1, source_target_pairs={{0,2},{1,3},{2,4},{3,5},{4,6},{5,7},{6,0},{7,1},{8,10},{9,11},{10,... | collective-permute-start | bytes 1572872 | tf_op jit(solution)/shard_map/ppermute | solution.py:384
  98.1 8.3 %collective-permute-start.19 = (bf16[16,64,128]{2,1,0:T(8,128)(2,1)S(1)}, bf16[16,64,128]{2,1,0:T(8,128)(2,1)S(1)}, u32[]{:S(2)}, u32[]{:S(2)}) collective-permute-start(bf16[16,64,128]{2,1,0:T(8,128)(2,1)S(1)} %slice.53), channel_id=1, source_target_pairs={{0,6},{1,7},{2,0},{3,1},{4,2},{5,3},{6,4},{7,5},{8,14},{9,15},{10,... | collective-permute-start | bytes 786440 | tf_op jit(solution)/shard_map/ppermute | solution.py:384
  100.8 10.6 %collective-permute-start.16 = (bf16[32,64,128]{2,1,0:T(8,128)(2,1)S(1)}, bf16[32,64,128]{2,1,0:T(8,128)(2,1)S(1)}, u32[]{:S(2)}, u32[]{:S(2)}) collective-permute-start(bf16[32,64,128]{2,1,0:T(8,128)(2,1)S(1)} %collective-permute-done.5.rest_2_), channel_id=1, source_target_pairs={{0,1},{1,0},{2,3},{3,2},{4,5},{5,4},{6,7},{7,6},{8,9},{9,8},{10,11... | collective-permute-start | bytes 1572872 | tf_op jit(solution)/shard_map/ppermute | solution.py:388
  100.8 10.6 %collective-permute-start.17 = (bf16[32,64,128]{2,1,0:T(8,128)(2,1)S(1)}, bf16[32,64,128]{2,1,0:T(8,128)(2,1)S(1)}, u32[]{:S(2)}, u32[]{:S(2)}) collective-permute-start(bf16[32,64,128]{2,1,0:T(8,128)(2,1)S(1)} %collective-permute-done.4.rest_4_), channel_id=1, source_target_pairs={{0,1},{1,0},{2,3},{3,2},{4,5},{5,4},{6,7},{7,6},{8,9},{9,8},{10,11... | collective-permute-start | bytes 1572872 | tf_op jit(solution)/shard_map/ppermute | solution.py:388
  101.3 9.4 %collective-permute-start.18 = (bf16[16,64,128]{2,1,0:T(8,128)(2,1)S(1)}, bf16[16,64,128]{2,1,0:T(8,128)(2,1)S(1)}, u32[]{:S(2)}, u32[]{:S(2)}) collective-permute-start(bf16[16,64,128]{2,1,0:T(8,128)(2,1)S(1)} %slice.52), channel_id=1, source_target_pairs={{0,2},{1,3},{2,4},{3,5},{4,6},{5,7},{6,0},{7,1},{8,10},{9,11},{10,... | collective-permute-start | bytes 786440 | tf_op jit(solution)/shard_map/ppermute | solution.py:384
  106.4 5.0 %collective-permute-start.21 = (bf16[16,64,128]{2,1,0:T(8,128)(2,1)S(1)}, bf16[16,64,128]{2,1,0:T(8,128)(2,1)}, u32[]{:S(2)}, u32[]{:S(2)}) collective-permute-start(bf16[16,64,128]{2,1,0:T(8,128)(2,1)S(1)} %collective-permute-done.19.rest_7_), channel_id=1, source_target_pairs={{0,1},{1,0},{2,3},{3,2},{4,5},{5,4},{6,7},{7,6},{8,9},{9,8},{10,11... | collective-permute-start | bytes 786440 | tf_op jit(solution)/shard_map/ppermute | solution.py:388
  142.5 12.1 %collective-permute-start.24 = (bf16[2,32,64,128]{3,2,1,0:T(8,128)(2,1)}, bf16[2,32,64,128]{3,2,1,0:T(8,128)(2,1)S(1)}, u32[]{:S(2)}, u32[]{:S(2)}) collective-permute-start(bf16[2,32,64,128]{3,2,1,0:T(8,128)(2,1)} %get-tuple-element.30), channel_id=1, source_target_pairs={{0,1},{1,0},{2,3},{3,2},{4,5},{5,4},{6,7},{7,6},{8,9},{9,8},{10,11... | collective-permute-start | bytes 3145736 | tf_op jit(solution)/shard_map/ppermute | solution.py:388
  146.8 3.2 %collective-permute-start.25 = (bf16[32,64,128]{2,1,0:T(8,128)(2,1)}, bf16[32,64,128]{2,1,0:T(8,128)(2,1)S(1)}, u32[]{:S(2)}, u32[]{:S(2)}) collective-permute-start(bf16[32,64,128]{2,1,0:T(8,128)(2,1)} %get-tuple-element.32), channel_id=1, source_target_pairs={{0,1},{1,0},{2,3},{3,2},{4,5},{5,4},{6,7},{7,6},{8,9},{9,8},{10,11... | collective-permute-start | bytes 1572872 | tf_op jit(solution)/shard_map/ppermute | solution.py:388
  146.9 17.7 %collective-permute-start.22 = (bf16[16,32,128]{2,1,0:T(8,128)(2,1)}, bf16[16,32,128]{2,1,0:T(8,128)(2,1)S(1)}, u32[]{:S(2)}, u32[]{:S(2)}) collective-permute-start(bf16[16,32,128]{2,1,0:T(8,128)(2,1)} %get-tuple-element.26), channel_id=1, source_target_pairs={{0,7},{1,6},{2,5},{3,4},{4,3},{5,2},{6,1},{7,0},{8,15},{9,14},{10,... | collective-permute-start | bytes 393224 | tf_op jit(solution)/shard_map/ppermute | solution.py:380
  146.9 28.4 %collective-permute-start.23 = (bf16[32,64,128]{2,1,0:T(8,128)(2,1)}, bf16[32,64,128]{2,1,0:T(8,128)(2,1)S(1)}, u32[]{:S(2)}, u32[]{:S(2)}) collective-permute-start(bf16[32,64,128]{2,1,0:T(8,128)(2,1)} %get-tuple-element.28), channel_id=1, source_target_pairs={{0,1},{1,0},{2,3},{3,2},{4,5},{5,4},{6,7},{7,6},{8,9},{9,8},{10,11... | collective-permute-start | bytes 1572872 | tf_op jit(solution)/shard_map/ppermute | solution.py:388
  151.3 9.9 %collective-permute-start.26 = (bf16[16,64,128]{2,1,0:T(8,128)(2,1)S(1)}, bf16[16,64,128]{2,1,0:T(8,128)(2,1)S(1)}, u32[]{:S(2)}, u32[]{:S(2)}) collective-permute-start(bf16[16,64,128]{2,1,0:T(8,128)(2,1)S(1)} %get-tuple-element.43), channel_id=1, source_target_pairs={{0,2},{1,3},{2,4},{3,5},{4,6},{5,7},{6,0},{7,1},{8,10},{9,11},{10,... | collective-permute-start | bytes 786440 | tf_op jit(solution)/shard_map/ppermute | solution.py:384
  151.4 9.8 %collective-permute-start.28 = (bf16[16,64,128]{2,1,0:T(8,128)(2,1)S(1)}, bf16[16,64,128]{2,1,0:T(8,128)(2,1)S(1)}, u32[]{:S(2)}, u32[]{:S(2)}) collective-permute-start(bf16[16,64,128]{2,1,0:T(8,128)(2,1)S(1)} %get-tuple-element.44), channel_id=1, source_target_pairs={{0,6},{1,7},{2,0},{3,1},{4,2},{5,3},{6,4},{7,5},{8,14},{9,15},{10,... | collective-permute-start | bytes 786440 | tf_op jit(solution)/shard_map/ppermute | solution.py:384
  161.4 13.9 %collective-permute-start.29 = (bf16[32,64,128]{2,1,0:T(8,128)(2,1)S(1)}, bf16[32,64,128]{2,1,0:T(8,128)(2,1)S(1)}, u32[]{:S(2)}, u32[]{:S(2)}) collective-permute-start(bf16[32,64,128]{2,1,0:T(8,128)(2,1)S(1)} %pad_maximum_fusion.1), channel_id=1, source_target_pairs={{0,6},{1,7},{2,0},{3,1},{4,2},{5,3},{6,4},{7,5},{8,14},{9,15},{10,... | collective-permute-start | bytes 1572872 | tf_op jit(solution)/shard_map/ppermute | solution.py:384
  164.5 14.1 %collective-permute-start.27 = (bf16[32,64,128]{2,1,0:T(8,128)(2,1)S(1)}, bf16[32,64,128]{2,1,0:T(8,128)(2,1)S(1)}, u32[]{:S(2)}, u32[]{:S(2)}) collective-permute-start(bf16[32,64,128]{2,1,0:T(8,128)(2,1)S(1)} %pad_maximum_fusion), channel_id=1, source_target_pairs={{0,2},{1,3},{2,4},{3,5},{4,6},{5,7},{6,0},{7,1},{8,10},{9,11},{10,... | collective-permute-start | bytes 1572872 | tf_op jit(solution)/shard_map/ppermute | solution.py:384
  165.3 21.3 %all-to-all-start.2 = ((bf16[32,32,128]{2,1,0:T(8,128)(2,1)}), bf16[32,32,128]{2,1,0:T(8,128)(2,1)S(1)}, u32[]{:S(2)}, u32[]{:S(2)}) async-start(bf16[32,32,128]{2,1,0:T(8,128)(2,1)} %pad_maximum_fusion.2), calls=%async_computation.2 | async-start | bytes 524288 | tf_op jit(solution)/shard_map/all_to_all | solution.py:376
  186.6 20.7 %all-to-all-start.3 = ((bf16[32,64,128]{2,1,0:T(8,128)(2,1)}), bf16[32,64,128]{2,1,0:T(8,128)(2,1)S(1)}, u32[]{:S(2)}, u32[]{:S(2)}) async-start(bf16[32,64,128]{2,1,0:T(8,128)(2,1)} %add_convert_fusion), calls=%async_computation.3 | async-start | bytes 1048576 | tf_op jit(solution)/shard_map/all_to_all | solution.py:376
  (19 other events, 160.1 us)
where the time goes:
time: 210 us
  Pallas kernels  55.2 us (26%)
  waiting for transfers between devices  53.8 us (26%)
  starting transfers between devices  47.1 us (22%)
  blocking collectives  43.5 us (21%)
  local copies, waits for them, and re-layouts  4.71 us (2%)
  other arithmetic  4.68 us (2%)
    all_to_all x1, blocking collectives, exchange(): lax.all_to_all(packed, 'seq', split_axis=0, concat_axis=0, tiled=True)  43.5 us
    pallas_call x1, Pallas kernels, student(): pl.pallas_call(student_kernel, out_shape=[half, half, one, one, two, two,...  30 us
    ppermute x14, waiting for transfers between devices, chip_shift(): lax.ppermute(x, 'blk', [(i, (i // 2 + by) % 4 * 2 + i % 2) for i in range...  27 us
    all_to_all x3, waiting for transfers between devices, exchange(): lax.all_to_all(packed, 'seq', split_axis=0, concat_axis=0, tiled=True)  21.4 us
    all_to_all x3, starting transfers between devices, exchange(): lax.all_to_all(packed, 'seq', split_axis=0, concat_axis=0, tiled=True)  19.1 us
    pallas_call x1, Pallas kernels, teacher(): pl.pallas_call(functools.partial(teacher_kernel, len(state), len(pieces),...  17.2 us
    ppermute x14, starting transfers between devices, chip_shift(): lax.ppermute(x, 'blk', [(i, (i // 2 + by) % 4 * 2 + i % 2) for i in range...  16.4 us
    ppermute x14, starting transfers between devices, swap_cores(): return lax.ppermute(x, 'blk', [(i, i ^ 1) for i in range(8)])  11.6 us
  transfers between devices with their start and end apart: 33, of which 13 were waited for; matrix products, arithmetic and copies ran while one was open for 3% of the time, Pallas kernels for 10%

commit v1 on v0

--- a/solution.py
+++ b/solution.py
@@ -35,25 +35,31 @@
     return jnp.dot(a, b, preferred_element_type=f32)
 
 
-def pack_kernel(count, *refs):
+def pack_kernel(count, with_frames, *refs):
     out_ref = refs[-1]
     for h in range(HEADS):
         for n in range(count):
             out_ref[h, n * SHARD:(n + 1) * SHARD, :] = refs[n][:, h * DH:(h + 1) * DH]
-        if len(refs) > count + 1:
-            out_ref[h, count * SHARD:, :] = refs[count][...]
-
-
-def pack(arrays, extra=()):
+    if with_frames:
+        column = lax.broadcasted_iota(jnp.int32, (EXTRA, DH), 1)
+        counts = jnp.zeros((EXTRA, DH), jnp.int32)
+        for k in range(SHARD):
+            counts = counts + (refs[count][0, k] <= column).astype(jnp.int32)
+        counts = counts.astype(f32).astype(bf16)
+        for h in range(HEADS):
+            out_ref[h, count * SHARD:, :] = counts
+
+
+def pack(arrays, frames=()):
     count = len(arrays)
-    rows = count * SHARD + sum(x.shape[0] for x in extra)
+    rows = count * SHARD + EXTRA * len(frames)
     return pl.pallas_call(
-        functools.partial(pack_kernel, count),
+        functools.partial(pack_kernel, count, len(frames) > 0),
         out_shape=jax.ShapeDtypeStruct((HEADS, rows, DH), bf16),
-        in_specs=[VMEM] * (count + len(extra)),
+        in_specs=[VMEM] * count + [SMEM] * len(frames),
         out_specs=VMEM,
         compiler_params=params(),
-    )(*arrays, *extra)
+    )(*arrays, *frames)
 
 
 def unpack_kernel(in_ref, *out_refs):
@@ -107,6 +113,15 @@
         after[2][...] = jnp.zeros((DH, ROWS), f32)
 
 
+def await_block(copies, i):
+    for k in range(8):
+
+        @pl.when(i == k)
+        def _():
+            for copy in copies[k:k + 1] if k < 6 else copies[2 * k - 6:2 * k - 4]:
+                copy.wait()
+
+
 def members_of(pieces):
     return sum(piece.shape[0] for piece in pieces)
 
@@ -167,10 +182,10 @@
     copies = load_pieces(pieces, held, sems)
     open_state(before, state)
     queries_t = take(own_ref, other_ref, 0, meta_ref).T
-    for copy in copies:
-        copy.wait()
 
     def step(i, _):
+        await_block(copies, 2 * i)
+        await_block(copies, 2 * i + 1)
         keys = keys_of(held, 2 * i, 2)
         values_t = values_of(held, 2 * i, 2).T
         for first in (0, HALF):
@@ -261,10 +276,9 @@
     bias = jnp.where((row > frames_of(tokens, meta_ref)) & (row < 7), hidden_bias, 0.0)
     qt_ref[:DH, :] = queries.T
     qt_ref[DH:, :] = bias.astype(bf16)
-    for copy in copies:
-        copy.wait()
 
     def forward(i, _):
+        await_block(copies, i)
         group = meta_ref[16 + i]
 
         def compute(first):
@@ -411,12 +425,9 @@
 ):
     blk = lax.axis_index("blk")
     seq = lax.axis_index("seq")
-    frame_ids = jnp.arange(DH, dtype=jnp.int32)
-    counts = jnp.sum((frame_index[0][:, None] <= frame_ids[None, :]).astype(f32), axis=0)
-    counts = jnp.broadcast_to(counts.astype(bf16), (EXTRA, DH))
     tie = lax.optimization_barrier
     arrays = (teacher_key, teacher_value, teacher_query, student_query)
-    moved = exchange(pack([x[0] for x in arrays], (counts,)))
+    moved = exchange(pack([x[0] for x in arrays], (frame_index,)))
     student_key, student_value, moved = tie((student_key, student_value, moved))
     student_kv = exchange(pack([student_key[0], student_value[0]]))
     teacher_kv = moved[:, :2 * SHARD]

time: 210 us -> 205 us (0.976)
  starting transfers between devices: 47.1 us -> 44.3 us
  transfers between devices with their start and end apart: 33 -> 33, of which waited for: 13 -> 15; matrix products, arithmetic and copies ran while one was open for 3% -> 3% of each run, Pallas kernels for 10% -> 10%
where the time goes in v1:
time: 205 us
  waiting for transfers between devices  54.8 us (27%)
  Pallas kernels  53.3 us (26%)
  starting transfers between devices  44.3 us (22%)
  blocking collectives  43.5 us (21%)
  local copies, waits for them, and re-layouts  4.09 us (2%)
  other arithmetic  3.95 us (2%)
    all_to_all x1, blocking collectives, exchange(): lax.all_to_all(packed, 'seq', split_axis=0, concat_axis=0, tiled=True)  43.5 us
    pallas_call x1, Pallas kernels, student(): pl.pallas_call(student_kernel, out_shape=[half, half, one, one, two, two,...  29 us
    ppermute x14, waiting for transfers between devices, chip_shift(): lax.ppermute(x, 'blk', [(i, (i // 2 + by) % 4 * 2 + i % 2) for i in range...  28 us
    all_to_all x3, waiting for transfers between devices, exchange(): lax.all_to_all(packed, 'seq', split_axis=0, concat_axis=0, tiled=True)  21.4 us
    all_to_all x3, starting transfers between devices, exchange(): lax.all_to_all(packed, 'seq', split_axis=0, concat_axis=0, tiled=True)  19 us
    pallas_call x1, Pallas kernels, teacher(): pl.pallas_call(functools.partial(teacher_kernel, len(state), len(pieces),...  16.3 us
    ppermute x14, starting transfers between devices, chip_shift(): lax.ppermute(x, 'blk', [(i, (i // 2 + by) % 4 * 2 + i % 2) for i in range...  15.5 us
    ppermute x14, starting transfers between devices, swap_cores(): return lax.ppermute(x, 'blk', [(i, i ^ 1) for i in range(8)])  9.76 us
  transfers between devices with their start and end apart: 33, of which 15 were waited for; matrix products, arithmetic and copies ran while one was open for 3% of the time, Pallas kernels for 10%

profile of v1, /device:TPU:32, one launch (start us, length us, event | category | flops | bytes accessed | tf_op | source)
XLA Modules:
  0.0 205.0 jit_solution(17493075236002325789)
XLA Ops:
  0.6 2.5 %shard_map.94 = bf16[32,144,128]{2,1,0:T(8,128)(2,1)} custom-call(bf16[32,4096]{1,0:T(8,128)(2,1)} %bitcast.38, bf16[32,4096]{1,0:T(8,128)(2,1)} %bitcast.39, bf16[32,4096]{1,0:T(8,128)(2,1)} %bitcast.40, bf16[32,4096]{1,0:T(8,128)(2,1)} %bitcast.41, s32[1,32]{1,0:T(1,128)} %refs_4_.1), custom_call_target="tpu_custom_call" | custom-call | tf_op jit(solution)/shard_map/pallas_call | solution.py:56
  3.1 43.5 %all_to_all.20 = bf16[32,144,128]{2,1,0:T(8,128)(2,1)S(1)} all-to-all(bf16[32,144,128]{2,1,0:T(8,128)(2,1)} %shard_map.94), channel_id=1, replica_groups=mesh['seq'=32,'blk'=8] {'seq'}, dimensions={0} | all-to-all | bytes 2359296 | tf_op jit(solution)/shard_map/all_to_all | solution.py:390
  46.7 1.6 collective-permute-start.9
  48.3 1.7 collective-permute-start.7
  50.0 1.9 shard_map.95
  52.0 4.6 %all-to-all-start.1 = ((bf16[32,64,128]{2,1,0:T(8,128)(2,1)}), bf16[32,64,128]{2,1,0:T(8,128)(2,1)S(1)}, u32[]{:S(2)}, u32[]{:S(2)}) async-start(bf16[32,64,128]{2,1,0:T(8,128)(2,1)} %shard_map.95), calls=%async_computation.1 | async-start | bytes 1048576 | tf_op jit(solution)/shard_map/all_to_all | solution.py:390
  57.4 1.7 collective-permute-start
  62.1 4.2 %collective-permute-done.1 = f32[8,128]{0,1:T(8,128)S(1)} collective-permute-done((f32[8,128]{0,1:T(8,128)S(1)}, f32[8,128]{0,1:T(8,128)S(1)}, u32[]{:S(2)}, u32[]{:S(2)}) %collective-permute-start.1) | collective-permute-done | bytes 4128 | tf_op jit(solution)/shard_map/ppermute | solution.py:398
  67.2 1.6 collective-permute-start.8
  68.8 3.2 %collective-permute-done.11.rest_6_ = bf16[16,64,128]{2,1,0:T(8,128)(2,1)S(1)} collective-permute-done((bf16[16,64,128]{2,1,0:T(8,128)(2,1)S(1)}, bf16[16,64,128]{2,1,0:T(8,128)(2,1)S(1)}, u32[]{:S(2)}, u32[]{:S(2)}) %collective-permute-start.11) | collective-permute-done | bytes 262176 | tf_op jit(solution)/shard_map/ppermute | solution.py:398
  71.9 1.2 collective-permute-start.13
  74.1 1.3 collective-permute-start.14
  77.3 1.5 collective-permute-start.5
  79.4 16.3 %shard_map.96.target_ref = bf16[128,1024]{1,0:T(8,128)(2,1)} custom-call(s32[24]{0:T(128)} %concatenate.20.meta_ref, bf16[16,64,128]{2,1,0:T(8,128)(2,1)} %get-tuple-element.46.own_ref, bf16[16,64,128]{2,1,0:T(8,128)(2,1)} %copy-done.13, bf16[32,64,128]{2,1,0:T(8,128)(2,1)} %copy-done.5, bf16[32,64,128]{2,1,0:T(8,128)(2,1)} %copy-done.10, ...), custom_call_target="tpu_custom_call" | custom-call | flops 15360000000 | bytes 4194304 | tf_op jit(solution)/shard_map/pallas_call | solution.py:210
  95.8 2.7 %collective-permute-start.19 = (bf16[16,64,128]{2,1,0:T(8,128)(2,1)S(1)}, bf16[16,64,128]{2,1,0:T(8,128)(2,1)S(1)}, u32[]{:S(2)}, u32[]{:S(2)}) collective-permute-start(bf16[16,64,128]{2,1,0:T(8,128)(2,1)S(1)} %slice.53), channel_id=1, source_target_pairs={{0,6},{1,7},{2,0},{3,1},{4,2},{5,3},{6,4},{7,5},{8,14},{9,15},{10,... | collective-permute-start | bytes 786440 | tf_op jit(solution)/shard_map/ppermute | solution.py:398
  99.1 5.1 %collective-permute-done.19.rest_7_ = bf16[16,64,128]{2,1,0:T(8,128)(2,1)S(1)} collective-permute-done((bf16[16,64,128]{2,1,0:T(8,128)(2,1)S(1)}, bf16[16,64,128]{2,1,0:T(8,128)(2,1)S(1)}, u32[]{:S(2)}, u32[]{:S(2)}) %collective-permute-start.19) | collective-permute-done | bytes 262176 | tf_op jit(solution)/shard_map/ppermute | solution.py:398
  104.1 4.3 %collective-permute-done.18.rest_6_ = bf16[16,64,128]{2,1,0:T(8,128)(2,1)S(1)} collective-permute-done((bf16[16,64,128]{2,1,0:T(8,128)(2,1)S(1)}, bf16[16,64,128]{2,1,0:T(8,128)(2,1)S(1)}, u32[]{:S(2)}, u32[]{:S(2)}) %collective-permute-start.18) | collective-permute-done | bytes 262176 | tf_op jit(solution)/shard_map/ppermute | solution.py:398
  110.2 29.0 %shard_map.97 = (bf16[16,32,128]{2,1,0:T(8,128)(2,1)}, bf16[16,32,128]{2,1,0:T(8,128)(2,1)}, bf16[32,64,128]{2,1,0:T(8,128)(2,1)}, bf16[32,64,128]{2,1,0:T(8,128...) custom-call(s32[24]{0:T(128)} %concatenate.19.meta_ref, ...), custom_call_target="tpu_custom_call" | custom-call | flops 25999998976 | bytes 10485760 | tf_op jit(solution)/shard_map/pallas_call | solution.py:364
  139.2 2.4 %collective-permute-start.24 = (bf16[2,32,64,128]{3,2,1,0:T(8,128)(2,1)}, bf16[2,32,64,128]{3,2,1,0:T(8,128)(2,1)S(1)}, u32[]{:S(2)}, u32[]{:S(2)}) collective-permute-start(bf16[2,32,64,128]{3,2,1,0:T(8,128)(2,1)} %get-tuple-element.30), channel_id=1, source_target_pairs={{0,1},{1,0},{2,3},{3,2},{4,5},{5,4},{6,7},{7,6},{8,9},{9,8},{10,11... | collective-permute-start | bytes 3145736 | tf_op jit(solution)/shard_map/ppermute | solution.py:402
  142.1 2.7 %collective-permute-done.25 = bf16[32,64,128]{2,1,0:T(8,128)(2,1)S(1)} collective-permute-done((bf16[32,64,128]{2,1,0:T(8,128)(2,1)}, bf16[32,64,128]{2,1,0:T(8,128)(2,1)S(1)}, u32[]{:S(2)}, u32[]{:S(2)}) %collective-permute-start.25) | collective-permute-done | bytes 524320 | tf_op jit(solution)/shard_map/ppermute | solution.py:402
  144.9 1.2 add_convert_fusion.1
  146.1 2.9 %collective-permute-start.26 = (bf16[16,64,128]{2,1,0:T(8,128)(2,1)S(1)}, bf16[16,64,128]{2,1,0:T(8,128)(2,1)S(1)}, u32[]{:S(2)}, u32[]{:S(2)}) collective-permute-start(bf16[16,64,128]{2,1,0:T(8,128)(2,1)S(1)} %get-tuple-element.43), channel_id=1, source_target_pairs={{0,2},{1,3},{2,4},{3,5},{4,6},{5,7},{6,0},{7,1},{8,10},{9,11},{10,... | collective-permute-start | bytes 786440 | tf_op jit(solution)/shard_map/ppermute | solution.py:398
  150.0 6.0 %collective-permute-done.26 = bf16[16,64,128]{2,1,0:T(8,128)(2,1)S(1)} collective-permute-done((bf16[16,64,128]{2,1,0:T(8,128)(2,1)S(1)}, bf16[16,64,128]{2,1,0:T(8,128)(2,1)S(1)}, u32[]{:S(2)}, u32[]{:S(2)}) %collective-permute-start.26) | collective-permute-done | bytes 262176 | tf_op jit(solution)/shard_map/ppermute | solution.py:398
  157.3 2.0 collective-permute-start.29
  160.3 9.8 %all-to-all-start.2 = ((bf16[32,32,128]{2,1,0:T(8,128)(2,1)}), bf16[32,32,128]{2,1,0:T(8,128)(2,1)S(1)}, u32[]{:S(2)}, u32[]{:S(2)}) async-start(bf16[32,32,128]{2,1,0:T(8,128)(2,1)} %pad_maximum_fusion.2), calls=%async_computation.2 | async-start | bytes 524288 | tf_op jit(solution)/shard_map/all_to_all | solution.py:390
  170.2 3.2 %collective-permute-done.27 = bf16[32,64,128]{2,1,0:T(8,128)(2,1)S(1)} collective-permute-done((bf16[32,64,128]{2,1,0:T(8,128)(2,1)S(1)}, bf16[32,64,128]{2,1,0:T(8,128)(2,1)S(1)}, u32[]{:S(2)}, u32[]{:S(2)}) %collective-permute-start.27) | collective-permute-done | bytes 524320 | tf_op jit(solution)/shard_map/ppermute | solution.py:398
  173.4 1.2 add_convert_fusion
  174.6 6.9 %all-to-all-done.2.in_ref = bf16[32,32,128]{2,1,0:T(8,128)(2,1)S(1)} async-done(((bf16[32,32,128]{2,1,0:T(8,128)(2,1)}), bf16[32,32,128]{2,1,0:T(8,128)(2,1)S(1)}, u32[]{:S(2)}, u32[]{:S(2)}) %all-to-all-start.2) | async-done | bytes 262176 | tf_op jit(solution)/shard_map/all_to_all | solution.py:390
  181.5 4.6 %all-to-all-start.3 = ((bf16[32,64,128]{2,1,0:T(8,128)(2,1)}), bf16[32,64,128]{2,1,0:T(8,128)(2,1)S(1)}, u32[]{:S(2)}, u32[]{:S(2)}) async-start(bf16[32,64,128]{2,1,0:T(8,128)(2,1)} %add_convert_fusion), calls=%async_computation.3 | async-start | bytes 1048576 | tf_op jit(solution)/shard_map/all_to_all | solution.py:390
  186.1 1.7 shard_map.98
  187.8 14.4 %all-to-all-done.3.in_ref = bf16[32,64,128]{2,1,0:T(8,128)(2,1)S(1)} async-done(((bf16[32,64,128]{2,1,0:T(8,128)(2,1)}), bf16[32,64,128]{2,1,0:T(8,128)(2,1)S(1)}, u32[]{:S(2)}, u32[]{:S(2)}) %all-to-all-start.3) | async-done | bytes 524320 | tf_op jit(solution)/shard_map/all_to_all | solution.py:390
  203.1 1.9 shard_map.99
  (102 shorter events, 15.0 us)
Async XLA Ops:
  46.7 13.9 %collective-permute-start.9 = (bf16[32,64,128]{2,1,0:T(8,128)(2,1)S(1)}, bf16[32,64,128]{2,1,0:T(8,128)(2,1)S(1)}, u32[]{:S(2)}, u32[]{:S(2)}) collective-permute-start(bf16[32,64,128]{2,1,0:T(8,128)(2,1)S(1)} %get-tuple-element.39.rest_0_), channel_id=1, source_target_pairs={{0,2},{1,3},{2,4},{3,5},{4,6},{5,7},{6,0},{7,1},{8,10},{9,11},{10,... | collective-permute-start | bytes 1572872 | tf_op jit(solution)/shard_map/ppermute | solution.py:398
  48.3 12.8 %collective-permute-start.7 = (bf16[32,64,128]{2,1,0:T(8,128)(2,1)S(1)}, bf16[32,64,128]{2,1,0:T(8,128)(2,1)}, u32[]{:S(2)}, u32[]{:S(2)}) collective-permute-start(bf16[32,64,128]{2,1,0:T(8,128)(2,1)S(1)} %get-tuple-element.39.rest_0_), channel_id=1, source_target_pairs={{0,6},{1,7},{2,0},{3,1},{4,2},{5,3},{6,4},{7,5},{8,14},{9,15},{10,... | collective-permute-start | bytes 1572872 | tf_op jit(solution)/shard_map/ppermute | solution.py:398
  52.0 25.2 %all-to-all-start.1 = ((bf16[32,64,128]{2,1,0:T(8,128)(2,1)}), bf16[32,64,128]{2,1,0:T(8,128)(2,1)S(1)}, u32[]{:S(2)}, u32[]{:S(2)}) async-start(bf16[32,64,128]{2,1,0:T(8,128)(2,1)} %shard_map.95), calls=%async_computation.1 | async-start | bytes 1048576 | tf_op jit(solution)/shard_map/all_to_all | solution.py:390
  57.3 9.8 %collective-permute-start.3 = (bf16[16,64,128]{2,1,0:T(8,128)(2,1)S(1)}, bf16[16,64,128]{2,1,0:T(8,128)(2,1)S(1)}, u32[]{:S(2)}, u32[]{:S(2)}) collective-permute-start(bf16[16,64,128]{2,1,0:T(8,128)(2,1)S(1)} %get-tuple-element.45), channel_id=1, source_target_pairs={{0,7},{1,6},{2,5},{3,4},{4,3},{5,2},{6,1},{7,0},{8,15},{9,14},{10,... | collective-permute-start | bytes 786440 | tf_op jit(solution)/shard_map/ppermute | solution.py:394
  57.4 2.6 %collective-permute-start = (f32[8,128]{0,1:T(8,128)S(1)}, f32[8,128]{0,1:T(8,128)S(1)}, u32[]{:S(2)}, u32[]{:S(2)}) collective-permute-start(f32[8,128]{0,1:T(8,128)S(1)} %broadcast_in_dim.21), channel_id=1, source_target_pairs={{0,1},{1,0},{2,3},{3,2},{4,5},{5,4},{6,7},{7,6},{8,9},{9,8},{10,11... | collective-permute-start | bytes 12296 | tf_op jit(solution)/shard_map/ppermute | solution.py:402
  60.1 6.3 %collective-permute-start.1 = (f32[8,128]{0,1:T(8,128)S(1)}, f32[8,128]{0,1:T(8,128)S(1)}, u32[]{:S(2)}, u32[]{:S(2)}) collective-permute-start(f32[8,128]{0,1:T(8,128)S(1)} %broadcast_add_fusion), channel_id=1, source_target_pairs={{0,2},{1,3},{2,4},{3,5},{4,6},{5,7},{6,0},{7,1},{8,10},{9,11},{10,... | collective-permute-start | bytes 12296 | tf_op jit(solution)/shard_map/ppermute | solution.py:398
  60.3 15.7 %collective-permute-start.6 = (bf16[32,64,128]{2,1,0:T(8,128)(2,1)S(1)}, bf16[32,64,128]{2,1,0:T(8,128)(2,1)S(1)}, u32[]{:S(2)}, u32[]{:S(2)}) collective-permute-start(bf16[32,64,128]{2,1,0:T(8,128)(2,1)S(1)} %get-tuple-element.39.rest_0_), channel_id=1, source_target_pairs={{0,1},{1,0},{2,3},{3,2},{4,5},{5,4},{6,7},{7,6},{8,9},{9,8},{10,11... | collective-permute-start | bytes 1572872 | tf_op jit(solution)/shard_map/ppermute | solution.py:402
  60.6 11.3 %collective-permute-start.11 = (bf16[16,64,128]{2,1,0:T(8,128)(2,1)S(1)}, bf16[16,64,128]{2,1,0:T(8,128)(2,1)S(1)}, u32[]{:S(2)}, u32[]{:S(2)}) collective-permute-start(bf16[16,64,128]{2,1,0:T(8,128)(2,1)S(1)} %slice.62), channel_id=1, source_target_pairs={{0,2},{1,3},{2,4},{3,5},{4,6},{5,7},{6,0},{7,1},{8,10},{9,11},{10,... | collective-permute-start | bytes 786440 | tf_op jit(solution)/shard_map/ppermute | solution.py:398
  61.1 16.2 %collective-permute-start.10 = (bf16[32,64,128]{2,1,0:T(8,128)(2,1)S(1)}, bf16[32,64,128]{2,1,0:T(8,128)(2,1)}, u32[]{:S(2)}, u32[]{:S(2)}) collective-permute-start(bf16[32,64,128]{2,1,0:T(8,128)(2,1)S(1)} %collective-permute-done.9.rest_4_), channel_id=1, source_target_pairs={{0,1},{1,0},{2,3},{3,2},{4,5},{5,4},{6,7},{7,6},{8,9},{9,8},{10,11... | collective-permute-start | bytes 1572872 | tf_op jit(solution)/shard_map/ppermute | solution.py:402
  66.3 7.7 %collective-permute-start.12 = (bf16[16,64,128]{2,1,0:T(8,128)(2,1)S(1)}, bf16[16,64,128]{2,1,0:T(8,128)(2,1)S(1)}, u32[]{:S(2)}, u32[]{:S(2)}) collective-permute-start(bf16[16,64,128]{2,1,0:T(8,128)(2,1)S(1)} %slice.63), channel_id=1, source_target_pairs={{0,6},{1,7},{2,0},{3,1},{4,2},{5,3},{6,4},{7,5},{8,14},{9,15},{10,... | collective-permute-start | bytes 786440 | tf_op jit(solution)/shard_map/ppermute | solution.py:398
  67.2 12.2 %collective-permute-start.8 = (bf16[32,64,128]{2,1,0:T(8,128)(2,1)}, bf16[32,64,128]{2,1,0:T(8,128)(2,1)}, u32[]{:S(2)}, u32[]{:S(2)}) collective-permute-start(bf16[32,64,128]{2,1,0:T(8,128)(2,1)} %collective-permute-done.7.rest_2_), channel_id=1, source_target_pairs={{0,1},{1,0},{2,3},{3,2},{4,5},{5,4},{6,7},{7,6},{8,9},{9,8},{10,11... | collective-permute-start | bytes 1572872 | tf_op jit(solution)/shard_map/ppermute | solution.py:402
  71.9 5.2 %collective-permute-start.13 = (bf16[16,64,128]{2,1,0:T(8,128)(2,1)S(1)}, bf16[16,64,128]{2,1,0:T(8,128)(2,1)}, u32[]{:S(2)}, u32[]{:S(2)}) collective-permute-start(bf16[16,64,128]{2,1,0:T(8,128)(2,1)S(1)} %collective-permute-done.11.rest_6_), channel_id=1, source_target_pairs={{0,1},{1,0},{2,3},{3,2},{4,5},{5,4},{6,7},{7,6},{8,9},{9,8},{10,11... | collective-permute-start | bytes 786440 | tf_op jit(solution)/shard_map/ppermute | solution.py:402
  74.1 4.7 %collective-permute-start.14 = (bf16[16,64,128]{2,1,0:T(8,128)(2,1)S(1)}, bf16[16,64,128]{2,1,0:T(8,128)(2,1)}, u32[]{:S(2)}, u32[]{:S(2)}) collective-permute-start(bf16[16,64,128]{2,1,0:T(8,128)(2,1)S(1)} %collective-permute-done.12.rest_7_), channel_id=1, source_target_pairs={{0,1},{1,0},{2,3},{3,2},{4,5},{5,4},{6,7},{7,6},{8,9},{9,8},{10,11... | collective-permute-start | bytes 786440 | tf_op jit(solution)/shard_map/ppermute | solution.py:402
  76.0 23.1 %collective-permute-start.2 = (f32[8,128]{0,1:T(8,128)S(1)}, f32[8,128]{0,1:T(8,128)S(1)}, u32[]{:S(2)}, u32[]{:S(2)}) collective-permute-start(f32[8,128]{0,1:T(8,128)S(1)} %fusion.9), channel_id=1, source_target_pairs={{0,4},{1,5},{2,6},{3,7},{4,0},{5,1},{6,2},{7,3},{8,12},{9,13},{10,... | collective-permute-start | bytes 12296 | tf_op jit(solution)/shard_map/ppermute | solution.py:398
  77.1 32.0 %collective-permute-start.15 = (bf16[32,64,128]{2,1,0:T(8,128)(2,1)S(1)}, bf16[32,64,128]{2,1,0:T(8,128)(2,1)}, u32[]{:S(2)}, u32[]{:S(2)}) collective-permute-start(bf16[32,64,128]{2,1,0:T(8,128)(2,1)S(1)} %all-to-all-done.1.rest_0_), channel_id=1, source_target_pairs={{0,1},{1,0},{2,3},{3,2},{4,5},{5,4},{6,7},{7,6},{8,9},{9,8},{10,11... | collective-permute-start | bytes 1572872 | tf_op jit(solution)/shard_map/ppermute | solution.py:402
  77.3 18.5 %collective-permute-start.5 = (bf16[32,64,128]{2,1,0:T(8,128)(2,1)S(1)}, bf16[32,64,128]{2,1,0:T(8,128)(2,1)S(1)}, u32[]{:S(2)}, u32[]{:S(2)}) collective-permute-start(bf16[32,64,128]{2,1,0:T(8,128)(2,1)S(1)} %all-to-all-done.1.rest_0_), channel_id=1, source_target_pairs={{0,6},{1,7},{2,0},{3,1},{4,2},{5,3},{6,4},{7,5},{8,14},{9,15},{10,... | collective-permute-start | bytes 1572872 | tf_op jit(solution)/shard_map/ppermute | solution.py:398
  78.8 17.0 %collective-permute-start.4 = (bf16[32,64,128]{2,1,0:T(8,128)(2,1)S(1)}, bf16[32,64,128]{2,1,0:T(8,128)(2,1)S(1)}, u32[]{:S(2)}, u32[]{:S(2)}) collective-permute-start(bf16[32,64,128]{2,1,0:T(8,128)(2,1)S(1)} %all-to-all-done.1.rest_0_), channel_id=1, source_target_pairs={{0,2},{1,3},{2,4},{3,5},{4,6},{5,7},{6,0},{7,1},{8,10},{9,11},{10,... | collective-permute-start | bytes 1572872 | tf_op jit(solution)/shard_map/ppermute | solution.py:398
  95.8 8.3 %collective-permute-start.19 = (bf16[16,64,128]{2,1,0:T(8,128)(2,1)S(1)}, bf16[16,64,128]{2,1,0:T(8,128)(2,1)S(1)}, u32[]{:S(2)}, u32[]{:S(2)}) collective-permute-start(bf16[16,64,128]{2,1,0:T(8,128)(2,1)S(1)} %slice.53), channel_id=1, source_target_pairs={{0,6},{1,7},{2,0},{3,1},{4,2},{5,3},{6,4},{7,5},{8,14},{9,15},{10,... | collective-permute-start | bytes 786440 | tf_op jit(solution)/shard_map/ppermute | solution.py:398
  98.5 10.6 %collective-permute-start.16 = (bf16[32,64,128]{2,1,0:T(8,128)(2,1)S(1)}, bf16[32,64,128]{2,1,0:T(8,128)(2,1)S(1)}, u32[]{:S(2)}, u32[]{:S(2)}) collective-permute-start(bf16[32,64,128]{2,1,0:T(8,128)(2,1)S(1)} %collective-permute-done.5.rest_2_), channel_id=1, source_target_pairs={{0,1},{1,0},{2,3},{3,2},{4,5},{5,4},{6,7},{7,6},{8,9},{9,8},{10,11... | collective-permute-start | bytes 1572872 | tf_op jit(solution)/shard_map/ppermute | solution.py:402
  98.5 10.6 %collective-permute-start.17 = (bf16[32,64,128]{2,1,0:T(8,128)(2,1)S(1)}, bf16[32,64,128]{2,1,0:T(8,128)(2,1)S(1)}, u32[]{:S(2)}, u32[]{:S(2)}) collective-permute-start(bf16[32,64,128]{2,1,0:T(8,128)(2,1)S(1)} %collective-permute-done.4.rest_4_), channel_id=1, source_target_pairs={{0,1},{1,0},{2,3},{3,2},{4,5},{5,4},{6,7},{7,6},{8,9},{9,8},{10,11... | collective-permute-start | bytes 1572872 | tf_op jit(solution)/shard_map/ppermute | solution.py:402
  99.1 9.4 %collective-permute-start.18 = (bf16[16,64,128]{2,1,0:T(8,128)(2,1)S(1)}, bf16[16,64,128]{2,1,0:T(8,128)(2,1)S(1)}, u32[]{:S(2)}, u32[]{:S(2)}) collective-permute-start(bf16[16,64,128]{2,1,0:T(8,128)(2,1)S(1)} %slice.52), channel_id=1, source_target_pairs={{0,2},{1,3},{2,4},{3,5},{4,6},{5,7},{6,0},{7,1},{8,10},{9,11},{10,... | collective-permute-start | bytes 786440 | tf_op jit(solution)/shard_map/ppermute | solution.py:398
  104.1 5.0 %collective-permute-start.21 = (bf16[16,64,128]{2,1,0:T(8,128)(2,1)S(1)}, bf16[16,64,128]{2,1,0:T(8,128)(2,1)}, u32[]{:S(2)}, u32[]{:S(2)}) collective-permute-start(bf16[16,64,128]{2,1,0:T(8,128)(2,1)S(1)} %collective-permute-done.19.rest_7_), channel_id=1, source_target_pairs={{0,1},{1,0},{2,3},{3,2},{4,5},{5,4},{6,7},{7,6},{8,9},{9,8},{10,11... | collective-permute-start | bytes 786440 | tf_op jit(solution)/shard_map/ppermute | solution.py:402
  139.2 10.3 %collective-permute-start.24 = (bf16[2,32,64,128]{3,2,1,0:T(8,128)(2,1)}, bf16[2,32,64,128]{3,2,1,0:T(8,128)(2,1)S(1)}, u32[]{:S(2)}, u32[]{:S(2)}) collective-permute-start(bf16[2,32,64,128]{3,2,1,0:T(8,128)(2,1)} %get-tuple-element.30), channel_id=1, source_target_pairs={{0,1},{1,0},{2,3},{3,2},{4,5},{5,4},{6,7},{7,6},{8,9},{9,8},{10,11... | collective-permute-start | bytes 3145736 | tf_op jit(solution)/shard_map/ppermute | solution.py:402
  141.6 3.2 %collective-permute-start.25 = (bf16[32,64,128]{2,1,0:T(8,128)(2,1)}, bf16[32,64,128]{2,1,0:T(8,128)(2,1)S(1)}, u32[]{:S(2)}, u32[]{:S(2)}) collective-permute-start(bf16[32,64,128]{2,1,0:T(8,128)(2,1)} %get-tuple-element.32), channel_id=1, source_target_pairs={{0,1},{1,0},{2,3},{3,2},{4,5},{5,4},{6,7},{7,6},{8,9},{9,8},{10,11... | collective-permute-start | bytes 1572872 | tf_op jit(solution)/shard_map/ppermute | solution.py:402
  141.7 17.8 %collective-permute-start.22 = (bf16[16,32,128]{2,1,0:T(8,128)(2,1)}, bf16[16,32,128]{2,1,0:T(8,128)(2,1)S(1)}, u32[]{:S(2)}, u32[]{:S(2)}) collective-permute-start(bf16[16,32,128]{2,1,0:T(8,128)(2,1)} %get-tuple-element.26), channel_id=1, source_target_pairs={{0,7},{1,6},{2,5},{3,4},{4,3},{5,2},{6,1},{7,0},{8,15},{9,14},{10,... | collective-permute-start | bytes 393224 | tf_op jit(solution)/shard_map/ppermute | solution.py:394
  141.7 28.4 %collective-permute-start.23 = (bf16[32,64,128]{2,1,0:T(8,128)(2,1)}, bf16[32,64,128]{2,1,0:T(8,128)(2,1)S(1)}, u32[]{:S(2)}, u32[]{:S(2)}) collective-permute-start(bf16[32,64,128]{2,1,0:T(8,128)(2,1)} %get-tuple-element.28), channel_id=1, source_target_pairs={{0,1},{1,0},{2,3},{3,2},{4,5},{5,4},{6,7},{7,6},{8,9},{9,8},{10,11... | collective-permute-start | bytes 1572872 | tf_op jit(solution)/shard_map/ppermute | solution.py:402
  146.1 9.9 %collective-permute-start.26 = (bf16[16,64,128]{2,1,0:T(8,128)(2,1)S(1)}, bf16[16,64,128]{2,1,0:T(8,128)(2,1)S(1)}, u32[]{:S(2)}, u32[]{:S(2)}) collective-permute-start(bf16[16,64,128]{2,1,0:T(8,128)(2,1)S(1)} %get-tuple-element.43), channel_id=1, source_target_pairs={{0,2},{1,3},{2,4},{3,5},{4,6},{5,7},{6,0},{7,1},{8,10},{9,11},{10,... | collective-permute-start | bytes 786440 | tf_op jit(solution)/shard_map/ppermute | solution.py:398
  149.0 8.1 %collective-permute-start.28 = (bf16[16,64,128]{2,1,0:T(8,128)(2,1)S(1)}, bf16[16,64,128]{2,1,0:T(8,128)(2,1)S(1)}, u32[]{:S(2)}, u32[]{:S(2)}) collective-permute-start(bf16[16,64,128]{2,1,0:T(8,128)(2,1)S(1)} %get-tuple-element.44), channel_id=1, source_target_pairs={{0,6},{1,7},{2,0},{3,1},{4,2},{5,3},{6,4},{7,5},{8,14},{9,15},{10,... | collective-permute-start | bytes 786440 | tf_op jit(solution)/shard_map/ppermute | solution.py:398
  157.3 12.9 %collective-permute-start.29 = (bf16[32,64,128]{2,1,0:T(8,128)(2,1)S(1)}, bf16[32,64,128]{2,1,0:T(8,128)(2,1)S(1)}, u32[]{:S(2)}, u32[]{:S(2)}) collective-permute-start(bf16[32,64,128]{2,1,0:T(8,128)(2,1)S(1)} %pad_maximum_fusion.1), channel_id=1, source_target_pairs={{0,6},{1,7},{2,0},{3,1},{4,2},{5,3},{6,4},{7,5},{8,14},{9,15},{10,... | collective-permute-start | bytes 1572872 | tf_op jit(solution)/shard_map/ppermute | solution.py:398
  159.3 14.1 %collective-permute-start.27 = (bf16[32,64,128]{2,1,0:T(8,128)(2,1)S(1)}, bf16[32,64,128]{2,1,0:T(8,128)(2,1)S(1)}, u32[]{:S(2)}, u32[]{:S(2)}) collective-permute-start(bf16[32,64,128]{2,1,0:T(8,128)(2,1)S(1)} %pad_maximum_fusion), channel_id=1, source_target_pairs={{0,2},{1,3},{2,4},{3,5},{4,6},{5,7},{6,0},{7,1},{8,10},{9,11},{10,... | collective-permute-start | bytes 1572872 | tf_op jit(solution)/shard_map/ppermute | solution.py:398
  160.3 21.2 %all-to-all-start.2 = ((bf16[32,32,128]{2,1,0:T(8,128)(2,1)}), bf16[32,32,128]{2,1,0:T(8,128)(2,1)S(1)}, u32[]{:S(2)}, u32[]{:S(2)}) async-start(bf16[32,32,128]{2,1,0:T(8,128)(2,1)} %pad_maximum_fusion.2), calls=%async_computation.2 | async-start | bytes 524288 | tf_op jit(solution)/shard_map/all_to_all | solution.py:390
  181.5 20.7 %all-to-all-start.3 = ((bf16[32,64,128]{2,1,0:T(8,128)(2,1)}), bf16[32,64,128]{2,1,0:T(8,128)(2,1)S(1)}, u32[]{:S(2)}, u32[]{:S(2)}) async-start(bf16[32,64,128]{2,1,0:T(8,128)(2,1)} %add_convert_fusion), calls=%async_computation.3 | async-start | bytes 1048576 | tf_op jit(solution)/shard_map/all_to_all | solution.py:390
  (19 other events, 155.1 us)

commit v2 on v1

--- a/solution.py
+++ b/solution.py
@@ -427,9 +427,10 @@
     seq = lax.axis_index("seq")
     tie = lax.optimization_barrier
     arrays = (teacher_key, teacher_value, teacher_query, student_query)
-    moved = exchange(pack([x[0] for x in arrays], (frame_index,)))
+    moved = exchange(pack([x[0] for x in arrays]))
     student_key, student_value, moved = tie((student_key, student_value, moved))
-    student_kv = exchange(pack([student_key[0], student_value[0]]))
+    student_moved = exchange(pack([student_key[0], student_value[0]], (frame_index,)))
+    student_kv = student_moved[:, :2 * SHARD]
     teacher_kv = moved[:, :2 * SHARD]
     early = seq < HALF_MEMBERS
     keep = jnp.where(early, 0, HALF_MEMBERS)
@@ -460,7 +461,7 @@
 
     teacher_after, teacher_before = chip_shift(teacher_kv, 3), chip_shift(teacher_kv, 1)
     student_after, student_before = chip_shift(student_kv, 3), chip_shift(student_kv, 1)
-    ends = frame_ends(moved[:, 4 * SHARD, :8])
+    ends = frame_ends(student_moved[:, 2 * SHARD, :8])
     meta = jnp.concatenate([ends, place[8:]])
     teacher_here = with_other_core([teacher_kv])
     teacher_near = near_pieces(teacher_after, teacher_before)

time: 205 us -> 212 us (1.034)
  waiting for transfers between devices: 54.8 us -> 64.7 us
  blocking collectives: 43.5 us -> 39.9 us
    ppermute x14, waiting for transfers between devices: 28 us -> 38.3 us  [chip_shift(): lax.ppermute(x, 'blk', [(i, (i // 2 + by) % 4 * 2 + i % 2) for i in range...]
    ppermute x14, starting transfers between devices: 15.5 us -> 20.6 us  [chip_shift(): lax.ppermute(x, 'blk', [(i, (i // 2 + by) % 4 * 2 + i % 2) for i in range...]
    ppermute x14, starting transfers between devices: 9.76 us -> 6.11 us  [swap_cores(): return lax.ppermute(x, 'blk', [(i, i ^ 1) for i in range(8)])]
    all_to_all x1, blocking collectives: 43.5 us -> 39.9 us  [exchange(): lax.all_to_all(packed, 'seq', split_axis=0, concat_axis=0, tiled=True)]
  transfers between devices with their start and end apart: 33 -> 33, of which waited for: 15 -> 15; matrix products, arithmetic and copies ran while one was open for 3% -> 3% of each run, Pallas kernels for 10% -> 9%
where the time goes in v2:
time: 212 us; the launch traced here: 210 us
  waiting for transfers between devices  64.7 us (31%)
  Pallas kernels  51.5 us (24%)
  starting transfers between devices  44.8 us (21%)
  blocking collectives  39.9 us (19%)
  local copies, waits for them, and re-layouts  4.02 us (2%)
  other arithmetic  3.94 us (2%)
    all_to_all x1, blocking collectives, exchange(): lax.all_to_all(packed, 'seq', split_axis=0, concat_axis=0, tiled=True)  39.9 us
    ppermute x14, waiting for transfers between devices, chip_shift(): lax.ppermute(x, 'blk', [(i, (i // 2 + by) % 4 * 2 + i % 2) for i in range...  38.3 us
    pallas_call x1, Pallas kernels, student(): pl.pallas_call(student_kernel, out_shape=[half, half, one, one, two, two,...  27.1 us
    all_to_all x3, waiting for transfers between devices, exchange(): lax.all_to_all(packed, 'seq', split_axis=0, concat_axis=0, tiled=True)  22.7 us
    ppermute x14, starting transfers between devices, chip_shift(): lax.ppermute(x, 'blk', [(i, (i // 2 + by) % 4 * 2 + i % 2) for i in range...  20.6 us
    all_to_all x3, starting transfers between devices, exchange(): lax.all_to_all(packed, 'seq', split_axis=0, concat_axis=0, tiled=True)  17.5 us
    pallas_call x1, Pallas kernels, teacher(): pl.pallas_call(functools.partial(teacher_kernel, len(state), len(pieces),...  16.3 us
    ppermute x14, starting transfers between devices, swap_cores(): return lax.ppermute(x, 'blk', [(i, i ^ 1) for i in range(8)])  6.11 us
  transfers between devices with their start and end apart: 33, of which 15 were waited for; matrix products, arithmetic and copies ran while one was open for 3% of the time, Pallas kernels for 9%

profile of v2, /device:TPU:32, one launch (start us, length us, event | category | flops | bytes accessed | tf_op | source)
XLA Modules:
  0.0 209.9 jit_solution(3962415331966450803)
XLA Ops:
  0.6 2.4 %shard_map.94 = bf16[32,128,128]{2,1,0:T(8,128)(2,1)} custom-call(bf16[32,4096]{1,0:T(8,128)(2,1)} %bitcast.41, bf16[32,4096]{1,0:T(8,128)(2,1)} %bitcast.42, bf16[32,4096]{1,0:T(8,128)(2,1)} %bitcast.43, bf16[32,4096]{1,0:T(8,128)(2,1)} %bitcast.44), custom_call_target="tpu_custom_call" | custom-call | tf_op jit(solution)/shard_map/pallas_call | solution.py:56
  3.0 39.9 %all_to_all.20 = bf16[32,128,128]{2,1,0:T(8,128)(2,1)S(1)} all-to-all(bf16[32,128,128]{2,1,0:T(8,128)(2,1)} %shard_map.94), channel_id=1, replica_groups=mesh['seq'=32,'blk'=8] {'seq'}, dimensions={0} | all-to-all | bytes 2097152 | tf_op jit(solution)/shard_map/all_to_all | solution.py:390
  42.9 2.0 shard_map.95
  44.9 5.2 %all-to-all-start.1 = ((bf16[32,80,128]{2,1,0:T(8,128)(2,1)}), bf16[32,80,128]{2,1,0:T(8,128)(2,1)S(1)}, u32[]{:S(2)}, u32[]{:S(2)}) async-start(bf16[32,80,128]{2,1,0:T(8,128)(2,1)} %shard_map.95), calls=%async_computation.1 | async-start | bytes 1310720 | tf_op jit(solution)/shard_map/all_to_all | solution.py:390
  50.2 1.6 collective-permute-start.9
  51.8 1.7 collective-permute-start.7
  54.3 12.1 %collective-permute-done.9.rest_4_ = bf16[32,64,128]{2,1,0:T(8,128)(2,1)S(1)} collective-permute-done((bf16[32,64,128]{2,1,0:T(8,128)(2,1)S(1)}, bf16[32,64,128]{2,1,0:T(8,128)(2,1)S(1)}, u32[]{:S(2)}, u32[]{:S(2)}) %collective-permute-start.9) | collective-permute-done | bytes 524320 | tf_op jit(solution)/shard_map/ppermute | solution.py:398
  66.5 3.4 %all-to-all-done.1 = bf16[32,80,128]{2,1,0:T(8,128)(2,1)S(1)} async-done(((bf16[32,80,128]{2,1,0:T(8,128)(2,1)}), bf16[32,80,128]{2,1,0:T(8,128)(2,1)S(1)}, u32[]{:S(2)}, u32[]{:S(2)}) %all-to-all-start.1) | async-done | bytes 655392 | tf_op jit(solution)/shard_map/all_to_all | solution.py:390
  71.6 2.8 %collective-permute-start.12 = (bf16[16,64,128]{2,1,0:T(8,128)(2,1)S(1)}, bf16[16,64,128]{2,1,0:T(8,128)(2,1)}, u32[]{:S(2)}, u32[]{:S(2)}) collective-permute-start(bf16[16,64,128]{2,1,0:T(8,128)(2,1)S(1)} %slice.69), channel_id=1, source_target_pairs={{0,6},{1,7},{2,0},{3,1},{4,2},{5,3},{6,4},{7,5},{8,14},{9,15},{10,... | collective-permute-start | bytes 786440 | tf_op jit(solution)/shard_map/ppermute | solution.py:398
  75.4 4.9 %collective-permute-done.12.rest_7_ = bf16[16,64,128]{2,1,0:T(8,128)(2,1)} collective-permute-done((bf16[16,64,128]{2,1,0:T(8,128)(2,1)S(1)}, bf16[16,64,128]{2,1,0:T(8,128)(2,1)}, u32[]{:S(2)}, u32[]{:S(2)}) %collective-permute-start.12) | collective-permute-done | bytes 262176 | tf_op jit(solution)/shard_map/ppermute | solution.py:398
  81.5 3.8 %collective-permute-start.5 = (bf16[32,64,128]{2,1,0:T(8,128)(2,1)S(1)}, bf16[32,64,128]{2,1,0:T(8,128)(2,1)S(1)}, u32[]{:S(2)}, u32[]{:S(2)}) collective-permute-start(bf16[32,64,128]{2,1,0:T(8,128)(2,1)S(1)} %slice.67.rest_0_), channel_id=1, source_target_pairs={{0,6},{1,7},{2,0},{3,1},{4,2},{5,3},{6,4},{7,5},{8,14},{9,15},{10,... | collective-permute-start | bytes 1572872 | tf_op jit(solution)/shard_map/ppermute | solution.py:398
  85.3 2.1 %collective-permute-start.2 = (f32[8,128]{0,1:T(8,128)S(1)}, f32[8,128]{0,1:T(8,128)S(1)}, u32[]{:S(2)}, u32[]{:S(2)}) collective-permute-start(f32[8,128]{0,1:T(8,128)S(1)} %fusion.10), channel_id=1, source_target_pairs={{0,4},{1,5},{2,6},{3,7},{4,0},{5,1},{6,2},{7,3},{8,12},{9,13},{10,... | collective-permute-start | bytes 12296 | tf_op jit(solution)/shard_map/ppermute | solution.py:398
  87.5 16.3 %shard_map.96.target_ref = bf16[128,1024]{1,0:T(8,128)(2,1)} custom-call(s32[24]{0:T(128)} %concatenate.20.meta_ref, bf16[16,64,128]{2,1,0:T(8,128)(2,1)} %get-tuple-element.46.own_ref, bf16[16,64,128]{2,1,0:T(8,128)(2,1)} %copy-done.13, bf16[32,64,128]{2,1,0:T(8,128)(2,1)} %copy-done.5, bf16[32,64,128]{2,1,0:T(8,128)(2,1)} %collective-permute-done.6.rest_1_, ...), custom_call_target="tpu_custom_call" | custom-call | flops 15360000000 | bytes 4194304 | tf_op jit(solution)/shard_map/pallas_call | solution.py:210
  106.7 6.3 %collective-permute-done.19.rest_7_ = bf16[16,64,128]{2,1,0:T(8,128)(2,1)S(1)} collective-permute-done((bf16[16,64,128]{2,1,0:T(8,128)(2,1)S(1)}, bf16[16,64,128]{2,1,0:T(8,128)(2,1)S(1)}, u32[]{:S(2)}, u32[]{:S(2)}) %collective-permute-start.19) | collective-permute-done | bytes 262176 | tf_op jit(solution)/shard_map/ppermute | solution.py:398
  113.0 2.5 %collective-permute-done.18.rest_6_ = bf16[16,64,128]{2,1,0:T(8,128)(2,1)} collective-permute-done((bf16[16,64,128]{2,1,0:T(8,128)(2,1)S(1)}, bf16[16,64,128]{2,1,0:T(8,128)(2,1)}, u32[]{:S(2)}, u32[]{:S(2)}) %collective-permute-start.18) | collective-permute-done | bytes 262176 | tf_op jit(solution)/shard_map/ppermute | solution.py:398
  116.1 1.2 collective-permute-done.20.rest_8_
  117.4 27.1 %shard_map.97 = (bf16[16,32,128]{2,1,0:T(8,128)(2,1)}, bf16[16,32,128]{2,1,0:T(8,128)(2,1)}, bf16[32,64,128]{2,1,0:T(8,128)(2,1)}, bf16[32,64,128]{2,1,0:T(8,128...) custom-call(s32[24]{0:T(128)} %concatenate.19.meta_ref, ...), custom_call_target="tpu_custom_call" | custom-call | flops 25999998976 | bytes 10485760 | tf_op jit(solution)/shard_map/pallas_call | solution.py:364
  144.5 4.2 %collective-permute-start.24 = (bf16[2,32,64,128]{3,2,1,0:T(8,128)(2,1)}, bf16[2,32,64,128]{3,2,1,0:T(8,128)(2,1)S(1)}, u32[]{:S(2)}, u32[]{:S(2)}) collective-permute-start(bf16[2,32,64,128]{3,2,1,0:T(8,128)(2,1)} %get-tuple-element.30), channel_id=1, source_target_pairs={{0,1},{1,0},{2,3},{3,2},{4,5},{5,4},{6,7},{7,6},{8,9},{9,8},{10,11... | collective-permute-start | bytes 3145736 | tf_op jit(solution)/shard_map/ppermute | solution.py:402
  149.5 2.5 %collective-permute-done.25 = bf16[32,64,128]{2,1,0:T(8,128)(2,1)S(1)} collective-permute-done((bf16[32,64,128]{2,1,0:T(8,128)(2,1)}, bf16[32,64,128]{2,1,0:T(8,128)(2,1)S(1)}, u32[]{:S(2)}, u32[]{:S(2)}) %collective-permute-start.25) | collective-permute-done | bytes 524320 | tf_op jit(solution)/shard_map/ppermute | solution.py:402
  152.0 1.2 add_convert_fusion.1
  153.3 2.0 collective-permute-start.26
  155.3 1.3 collective-permute-start.28
  157.1 6.0 %collective-permute-done.26 = bf16[16,64,128]{2,1,0:T(8,128)(2,1)S(1)} collective-permute-done((bf16[16,64,128]{2,1,0:T(8,128)(2,1)S(1)}, bf16[16,64,128]{2,1,0:T(8,128)(2,1)S(1)}, u32[]{:S(2)}, u32[]{:S(2)}) %collective-permute-start.26) | collective-permute-done | bytes 262176 | tf_op jit(solution)/shard_map/ppermute | solution.py:398
  163.6 2.9 %collective-permute-start.29 = (bf16[32,64,128]{2,1,0:T(8,128)(2,1)S(1)}, bf16[32,64,128]{2,1,0:T(8,128)(2,1)S(1)}, u32[]{:S(2)}, u32[]{:S(2)}) collective-permute-start(bf16[32,64,128]{2,1,0:T(8,128)(2,1)S(1)} %pad_maximum_fusion.1), channel_id=1, source_target_pairs={{0,6},{1,7},{2,0},{3,1},{4,2},{5,3},{6,4},{7,5},{8,14},{9,15},{10,... | collective-permute-start | bytes 1572872 | tf_op jit(solution)/shard_map/ppermute | solution.py:398
  167.3 7.8 %all-to-all-start.2 = ((bf16[32,32,128]{2,1,0:T(8,128)(2,1)}), bf16[32,32,128]{2,1,0:T(8,128)(2,1)S(1)}, u32[]{:S(2)}, u32[]{:S(2)}) async-start(bf16[32,32,128]{2,1,0:T(8,128)(2,1)} %pad_maximum_fusion.2), calls=%async_computation.2 | async-start | bytes 524288 | tf_op jit(solution)/shard_map/all_to_all | solution.py:390
  175.1 1.9 collective-permute-done.29
  177.0 3.5 %collective-permute-done.27 = bf16[32,64,128]{2,1,0:T(8,128)(2,1)S(1)} collective-permute-done((bf16[32,64,128]{2,1,0:T(8,128)(2,1)S(1)}, bf16[32,64,128]{2,1,0:T(8,128)(2,1)S(1)}, u32[]{:S(2)}, u32[]{:S(2)}) %collective-permute-start.27) | collective-permute-done | bytes 524320 | tf_op jit(solution)/shard_map/ppermute | solution.py:398
  181.7 4.8 %all-to-all-done.2.in_ref = bf16[32,32,128]{2,1,0:T(8,128)(2,1)S(1)} async-done(((bf16[32,32,128]{2,1,0:T(8,128)(2,1)}), bf16[32,32,128]{2,1,0:T(8,128)(2,1)S(1)}, u32[]{:S(2)}, u32[]{:S(2)}) %all-to-all-start.2) | async-done | bytes 262176 | tf_op jit(solution)/shard_map/all_to_all | solution.py:390
  186.5 4.6 %all-to-all-start.3 = ((bf16[32,64,128]{2,1,0:T(8,128)(2,1)}), bf16[32,64,128]{2,1,0:T(8,128)(2,1)S(1)}, u32[]{:S(2)}, u32[]{:S(2)}) async-start(bf16[32,64,128]{2,1,0:T(8,128)(2,1)} %add_convert_fusion), calls=%async_computation.3 | async-start | bytes 1048576 | tf_op jit(solution)/shard_map/all_to_all | solution.py:390
  191.1 1.7 shard_map.98
  192.8 14.4 %all-to-all-done.3.in_ref = bf16[32,64,128]{2,1,0:T(8,128)(2,1)S(1)} async-done(((bf16[32,64,128]{2,1,0:T(8,128)(2,1)}), bf16[32,64,128]{2,1,0:T(8,128)(2,1)S(1)}, u32[]{:S(2)}, u32[]{:S(2)}) %all-to-all-start.3) | async-done | bytes 524320 | tf_op jit(solution)/shard_map/all_to_all | solution.py:390
  208.0 1.9 shard_map.99
  (99 shorter events, 12.8 us)
Async XLA Ops:
  44.9 25.0 %all-to-all-start.1 = ((bf16[32,80,128]{2,1,0:T(8,128)(2,1)}), bf16[32,80,128]{2,1,0:T(8,128)(2,1)S(1)}, u32[]{:S(2)}, u32[]{:S(2)}) async-start(bf16[32,80,128]{2,1,0:T(8,128)(2,1)} %shard_map.95), calls=%async_computation.1 | async-start | bytes 1310720 | tf_op jit(solution)/shard_map/all_to_all | solution.py:390
  50.2 16.2 %collective-permute-start.9 = (bf16[32,64,128]{2,1,0:T(8,128)(2,1)S(1)}, bf16[32,64,128]{2,1,0:T(8,128)(2,1)S(1)}, u32[]{:S(2)}, u32[]{:S(2)}) collective-permute-start(bf16[32,64,128]{2,1,0:T(8,128)(2,1)S(1)} %get-tuple-element.41.rest_0_), channel_id=1, source_target_pairs={{0,2},{1,3},{2,4},{3,5},{4,6},{5,7},{6,0},{7,1},{8,10},{9,11},{10,... | collective-permute-start | bytes 1572872 | tf_op jit(solution)/shard_map/ppermute | solution.py:398
  51.8 18.8 %collective-permute-start.7 = (bf16[32,64,128]{2,1,0:T(8,128)(2,1)S(1)}, bf16[32,64,128]{2,1,0:T(8,128)(2,1)}, u32[]{:S(2)}, u32[]{:S(2)}) collective-permute-start(bf16[32,64,128]{2,1,0:T(8,128)(2,1)S(1)} %get-tuple-element.41.rest_0_), channel_id=1, source_target_pairs={{0,6},{1,7},{2,0},{3,1},{4,2},{5,3},{6,4},{7,5},{8,14},{9,15},{10,... | collective-permute-start | bytes 1572872 | tf_op jit(solution)/shard_map/ppermute | solution.py:398
  54.3 20.1 %collective-permute-start.3 = (bf16[16,64,128]{2,1,0:T(8,128)(2,1)S(1)}, bf16[16,64,128]{2,1,0:T(8,128)(2,1)S(1)}, u32[]{:S(2)}, u32[]{:S(2)}) collective-permute-start(bf16[16,64,128]{2,1,0:T(8,128)(2,1)S(1)} %get-tuple-element.45), channel_id=1, source_target_pairs={{0,7},{1,6},{2,5},{3,4},{4,3},{5,2},{6,1},{7,0},{8,15},{9,14},{10,... | collective-permute-start | bytes 786440 | tf_op jit(solution)/shard_map/ppermute | solution.py:394
  66.4 8.9 %collective-permute-start.11 = (bf16[16,64,128]{2,1,0:T(8,128)(2,1)S(1)}, bf16[16,64,128]{2,1,0:T(8,128)(2,1)S(1)}, u32[]{:S(2)}, u32[]{:S(2)}) collective-permute-start(bf16[16,64,128]{2,1,0:T(8,128)(2,1)S(1)} %slice.68), channel_id=1, source_target_pairs={{0,2},{1,3},{2,4},{3,5},{4,6},{5,7},{6,0},{7,1},{8,10},{9,11},{10,... | collective-permute-start | bytes 786440 | tf_op jit(solution)/shard_map/ppermute | solution.py:398
  70.0 4.4 %collective-permute-start = (f32[8,128]{0,1:T(8,128)S(1)}, f32[8,128]{0,1:T(8,128)S(1)}, u32[]{:S(2)}, u32[]{:S(2)}) collective-permute-start(f32[8,128]{0,1:T(8,128)S(1)} %broadcast_in_dim.21), channel_id=1, source_target_pairs={{0,1},{1,0},{2,3},{3,2},{4,5},{5,4},{6,7},{7,6},{8,9},{9,8},{10,11... | collective-permute-start | bytes 12296 | tf_op jit(solution)/shard_map/ppermute | solution.py:402
  70.1 11.4 %collective-permute-start.6 = (bf16[32,64,128]{2,1,0:T(8,128)(2,1)S(1)}, bf16[32,64,128]{2,1,0:T(8,128)(2,1)}, u32[]{:S(2)}, u32[]{:S(2)}) collective-permute-start(bf16[32,64,128]{2,1,0:T(8,128)(2,1)S(1)} %get-tuple-element.41.rest_0_), channel_id=1, source_target_pairs={{0,1},{1,0},{2,3},{3,2},{4,5},{5,4},{6,7},{7,6},{8,9},{9,8},{10,11... | collective-permute-start | bytes 1572872 | tf_op jit(solution)/shard_map/ppermute | solution.py:402
  71.6 8.7 %collective-permute-start.12 = (bf16[16,64,128]{2,1,0:T(8,128)(2,1)S(1)}, bf16[16,64,128]{2,1,0:T(8,128)(2,1)}, u32[]{:S(2)}, u32[]{:S(2)}) collective-permute-start(bf16[16,64,128]{2,1,0:T(8,128)(2,1)S(1)} %slice.69), channel_id=1, source_target_pairs={{0,6},{1,7},{2,0},{3,1},{4,2},{5,3},{6,4},{7,5},{8,14},{9,15},{10,... | collective-permute-start | bytes 786440 | tf_op jit(solution)/shard_map/ppermute | solution.py:398
  74.4 13.1 %collective-permute-start.10 = (bf16[32,64,128]{2,1,0:T(8,128)(2,1)S(1)}, bf16[32,64,128]{2,1,0:T(8,128)(2,1)}, u32[]{:S(2)}, u32[]{:S(2)}) collective-permute-start(bf16[32,64,128]{2,1,0:T(8,128)(2,1)S(1)} %collective-permute-done.9.rest_4_), channel_id=1, source_target_pairs={{0,1},{1,0},{2,3},{3,2},{4,5},{5,4},{6,7},{7,6},{8,9},{9,8},{10,11... | collective-permute-start | bytes 1572872 | tf_op jit(solution)/shard_map/ppermute | solution.py:402
  74.4 13.0 %collective-permute-start.8 = (bf16[32,64,128]{2,1,0:T(8,128)(2,1)}, bf16[32,64,128]{2,1,0:T(8,128)(2,1)}, u32[]{:S(2)}, u32[]{:S(2)}) collective-permute-start(bf16[32,64,128]{2,1,0:T(8,128)(2,1)} %collective-permute-done.7.rest_2_), channel_id=1, source_target_pairs={{0,1},{1,0},{2,3},{3,2},{4,5},{5,4},{6,7},{7,6},{8,9},{9,8},{10,11... | collective-permute-start | bytes 1572872 | tf_op jit(solution)/shard_map/ppermute | solution.py:402
  75.4 5.5 %collective-permute-start.1 = (f32[8,128]{0,1:T(8,128)S(1)}, f32[8,128]{0,1:T(8,128)S(1)}, u32[]{:S(2)}, u32[]{:S(2)}) collective-permute-start(f32[8,128]{0,1:T(8,128)S(1)} %broadcast_add_fusion), channel_id=1, source_target_pairs={{0,2},{1,3},{2,4},{3,5},{4,6},{5,7},{6,0},{7,1},{8,10},{9,11},{10,... | collective-permute-start | bytes 12296 | tf_op jit(solution)/shard_map/ppermute | solution.py:398
  80.2 5.1 %collective-permute-start.13 = (bf16[16,64,128]{2,1,0:T(8,128)(2,1)S(1)}, bf16[16,64,128]{2,1,0:T(8,128)(2,1)}, u32[]{:S(2)}, u32[]{:S(2)}) collective-permute-start(bf16[16,64,128]{2,1,0:T(8,128)(2,1)S(1)} %collective-permute-done.11.rest_6_), channel_id=1, source_target_pairs={{0,1},{1,0},{2,3},{3,2},{4,5},{5,4},{6,7},{7,6},{8,9},{9,8},{10,11... | collective-permute-start | bytes 786440 | tf_op jit(solution)/shard_map/ppermute | solution.py:402
  80.8 4.5 %collective-permute-start.14 = (bf16[16,64,128]{2,1,0:T(8,128)(2,1)}, bf16[16,64,128]{2,1,0:T(8,128)(2,1)}, u32[]{:S(2)}, u32[]{:S(2)}) collective-permute-start(bf16[16,64,128]{2,1,0:T(8,128)(2,1)} %collective-permute-done.12.rest_7_), channel_id=1, source_target_pairs={{0,1},{1,0},{2,3},{3,2},{4,5},{5,4},{6,7},{7,6},{8,9},{9,8},{10,11... | collective-permute-start | bytes 786440 | tf_op jit(solution)/shard_map/ppermute | solution.py:402
  81.5 22.4 %collective-permute-start.5 = (bf16[32,64,128]{2,1,0:T(8,128)(2,1)S(1)}, bf16[32,64,128]{2,1,0:T(8,128)(2,1)S(1)}, u32[]{:S(2)}, u32[]{:S(2)}) collective-permute-start(bf16[32,64,128]{2,1,0:T(8,128)(2,1)S(1)} %slice.67.rest_0_), channel_id=1, source_target_pairs={{0,6},{1,7},{2,0},{3,1},{4,2},{5,3},{6,4},{7,5},{8,14},{9,15},{10,... | collective-permute-start | bytes 1572872 | tf_op jit(solution)/shard_map/ppermute | solution.py:398
  85.3 18.7 %collective-permute-start.4 = (bf16[32,64,128]{2,1,0:T(8,128)(2,1)S(1)}, bf16[32,64,128]{2,1,0:T(8,128)(2,1)S(1)}, u32[]{:S(2)}, u32[]{:S(2)}) collective-permute-start(bf16[32,64,128]{2,1,0:T(8,128)(2,1)S(1)} %slice.67.rest_0_), channel_id=1, source_target_pairs={{0,2},{1,3},{2,4},{3,5},{4,6},{5,7},{6,0},{7,1},{8,10},{9,11},{10,... | collective-permute-start | bytes 1572872 | tf_op jit(solution)/shard_map/ppermute | solution.py:398
  85.3 20.4 %collective-permute-start.2 = (f32[8,128]{0,1:T(8,128)S(1)}, f32[8,128]{0,1:T(8,128)S(1)}, u32[]{:S(2)}, u32[]{:S(2)}) collective-permute-start(f32[8,128]{0,1:T(8,128)S(1)} %fusion.10), channel_id=1, source_target_pairs={{0,4},{1,5},{2,6},{3,7},{4,0},{5,1},{6,2},{7,3},{8,12},{9,13},{10,... | collective-permute-start | bytes 12296 | tf_op jit(solution)/shard_map/ppermute | solution.py:398
  103.8 12.2 %collective-permute-start.15 = (bf16[32,64,128]{2,1,0:T(8,128)(2,1)S(1)}, bf16[32,64,128]{2,1,0:T(8,128)(2,1)S(1)}, u32[]{:S(2)}, u32[]{:S(2)}) collective-permute-start(bf16[32,64,128]{2,1,0:T(8,128)(2,1)S(1)} %slice.67.rest_0_), channel_id=1, source_target_pairs={{0,1},{1,0},{2,3},{3,2},{4,5},{5,4},{6,7},{7,6},{8,9},{9,8},{10,11... | collective-permute-start | bytes 1572872 | tf_op jit(solution)/shard_map/ppermute | solution.py:402
  104.0 9.0 %collective-permute-start.19 = (bf16[16,64,128]{2,1,0:T(8,128)(2,1)S(1)}, bf16[16,64,128]{2,1,0:T(8,128)(2,1)S(1)}, u32[]{:S(2)}, u32[]{:S(2)}) collective-permute-start(bf16[16,64,128]{2,1,0:T(8,128)(2,1)S(1)} %slice.57), channel_id=1, source_target_pairs={{0,6},{1,7},{2,0},{3,1},{4,2},{5,3},{6,4},{7,5},{8,14},{9,15},{10,... | collective-permute-start | bytes 786440 | tf_op jit(solution)/shard_map/ppermute | solution.py:398
  105.2 10.9 %collective-permute-start.16 = (bf16[32,64,128]{2,1,0:T(8,128)(2,1)S(1)}, bf16[32,64,128]{2,1,0:T(8,128)(2,1)S(1)}, u32[]{:S(2)}, u32[]{:S(2)}) collective-permute-start(bf16[32,64,128]{2,1,0:T(8,128)(2,1)S(1)} %collective-permute-done.5.rest_2_), channel_id=1, source_target_pairs={{0,1},{1,0},{2,3},{3,2},{4,5},{5,4},{6,7},{7,6},{8,9},{9,8},{10,11... | collective-permute-start | bytes 1572872 | tf_op jit(solution)/shard_map/ppermute | solution.py:402
  105.4 10.7 %collective-permute-start.17 = (bf16[32,64,128]{2,1,0:T(8,128)(2,1)S(1)}, bf16[32,64,128]{2,1,0:T(8,128)(2,1)S(1)}, u32[]{:S(2)}, u32[]{:S(2)}) collective-permute-start(bf16[32,64,128]{2,1,0:T(8,128)(2,1)S(1)} %collective-permute-done.4.rest_4_), channel_id=1, source_target_pairs={{0,1},{1,0},{2,3},{3,2},{4,5},{5,4},{6,7},{7,6},{8,9},{9,8},{10,11... | collective-permute-start | bytes 1572872 | tf_op jit(solution)/shard_map/ppermute | solution.py:402
  105.7 9.7 %collective-permute-start.18 = (bf16[16,64,128]{2,1,0:T(8,128)(2,1)S(1)}, bf16[16,64,128]{2,1,0:T(8,128)(2,1)}, u32[]{:S(2)}, u32[]{:S(2)}) collective-permute-start(bf16[16,64,128]{2,1,0:T(8,128)(2,1)S(1)} %slice.56), channel_id=1, source_target_pairs={{0,2},{1,3},{2,4},{3,5},{4,6},{5,7},{6,0},{7,1},{8,10},{9,11},{10,... | collective-permute-start | bytes 786440 | tf_op jit(solution)/shard_map/ppermute | solution.py:398
  113.0 3.1 %collective-permute-start.21 = (bf16[16,64,128]{2,1,0:T(8,128)(2,1)S(1)}, bf16[16,64,128]{2,1,0:T(8,128)(2,1)}, u32[]{:S(2)}, u32[]{:S(2)}) collective-permute-start(bf16[16,64,128]{2,1,0:T(8,128)(2,1)S(1)} %collective-permute-done.19.rest_7_), channel_id=1, source_target_pairs={{0,1},{1,0},{2,3},{3,2},{4,5},{5,4},{6,7},{7,6},{8,9},{9,8},{10,11... | collective-permute-start | bytes 786440 | tf_op jit(solution)/shard_map/ppermute | solution.py:402
  144.5 12.1 %collective-permute-start.24 = (bf16[2,32,64,128]{3,2,1,0:T(8,128)(2,1)}, bf16[2,32,64,128]{3,2,1,0:T(8,128)(2,1)S(1)}, u32[]{:S(2)}, u32[]{:S(2)}) collective-permute-start(bf16[2,32,64,128]{3,2,1,0:T(8,128)(2,1)} %get-tuple-element.30), channel_id=1, source_target_pairs={{0,1},{1,0},{2,3},{3,2},{4,5},{5,4},{6,7},{7,6},{8,9},{9,8},{10,11... | collective-permute-start | bytes 3145736 | tf_op jit(solution)/shard_map/ppermute | solution.py:402
  148.8 3.2 %collective-permute-start.25 = (bf16[32,64,128]{2,1,0:T(8,128)(2,1)}, bf16[32,64,128]{2,1,0:T(8,128)(2,1)S(1)}, u32[]{:S(2)}, u32[]{:S(2)}) collective-permute-start(bf16[32,64,128]{2,1,0:T(8,128)(2,1)} %get-tuple-element.32), channel_id=1, source_target_pairs={{0,1},{1,0},{2,3},{3,2},{4,5},{5,4},{6,7},{7,6},{8,9},{9,8},{10,11... | collective-permute-start | bytes 1572872 | tf_op jit(solution)/shard_map/ppermute | solution.py:402
  148.9 17.7 %collective-permute-start.22 = (bf16[16,32,128]{2,1,0:T(8,128)(2,1)}, bf16[16,32,128]{2,1,0:T(8,128)(2,1)S(1)}, u32[]{:S(2)}, u32[]{:S(2)}) collective-permute-start(bf16[16,32,128]{2,1,0:T(8,128)(2,1)} %get-tuple-element.26), channel_id=1, source_target_pairs={{0,7},{1,6},{2,5},{3,4},{4,3},{5,2},{6,1},{7,0},{8,15},{9,14},{10,... | collective-permute-start | bytes 393224 | tf_op jit(solution)/shard_map/ppermute | solution.py:394
  149.4 25.7 %collective-permute-start.23 = (bf16[32,64,128]{2,1,0:T(8,128)(2,1)}, bf16[32,64,128]{2,1,0:T(8,128)(2,1)S(1)}, u32[]{:S(2)}, u32[]{:S(2)}) collective-permute-start(bf16[32,64,128]{2,1,0:T(8,128)(2,1)} %get-tuple-element.28), channel_id=1, source_target_pairs={{0,1},{1,0},{2,3},{3,2},{4,5},{5,4},{6,7},{7,6},{8,9},{9,8},{10,11... | collective-permute-start | bytes 1572872 | tf_op jit(solution)/shard_map/ppermute | solution.py:402
  153.3 9.9 %collective-permute-start.26 = (bf16[16,64,128]{2,1,0:T(8,128)(2,1)S(1)}, bf16[16,64,128]{2,1,0:T(8,128)(2,1)S(1)}, u32[]{:S(2)}, u32[]{:S(2)}) collective-permute-start(bf16[16,64,128]{2,1,0:T(8,128)(2,1)S(1)} %get-tuple-element.43), channel_id=1, source_target_pairs={{0,2},{1,3},{2,4},{3,5},{4,6},{5,7},{6,0},{7,1},{8,10},{9,11},{10,... | collective-permute-start | bytes 786440 | tf_op jit(solution)/shard_map/ppermute | solution.py:398
  155.3 8.1 %collective-permute-start.28 = (bf16[16,64,128]{2,1,0:T(8,128)(2,1)S(1)}, bf16[16,64,128]{2,1,0:T(8,128)(2,1)S(1)}, u32[]{:S(2)}, u32[]{:S(2)}) collective-permute-start(bf16[16,64,128]{2,1,0:T(8,128)(2,1)S(1)} %get-tuple-element.44), channel_id=1, source_target_pairs={{0,6},{1,7},{2,0},{3,1},{4,2},{5,3},{6,4},{7,5},{8,14},{9,15},{10,... | collective-permute-start | bytes 786440 | tf_op jit(solution)/shard_map/ppermute | solution.py:398
  163.6 13.4 %collective-permute-start.29 = (bf16[32,64,128]{2,1,0:T(8,128)(2,1)S(1)}, bf16[32,64,128]{2,1,0:T(8,128)(2,1)S(1)}, u32[]{:S(2)}, u32[]{:S(2)}) collective-permute-start(bf16[32,64,128]{2,1,0:T(8,128)(2,1)S(1)} %pad_maximum_fusion.1), channel_id=1, source_target_pairs={{0,6},{1,7},{2,0},{3,1},{4,2},{5,3},{6,4},{7,5},{8,14},{9,15},{10,... | collective-permute-start | bytes 1572872 | tf_op jit(solution)/shard_map/ppermute | solution.py:398
  166.5 14.1 %collective-permute-start.27 = (bf16[32,64,128]{2,1,0:T(8,128)(2,1)S(1)}, bf16[32,64,128]{2,1,0:T(8,128)(2,1)S(1)}, u32[]{:S(2)}, u32[]{:S(2)}) collective-permute-start(bf16[32,64,128]{2,1,0:T(8,128)(2,1)S(1)} %pad_maximum_fusion), channel_id=1, source_target_pairs={{0,2},{1,3},{2,4},{3,5},{4,6},{5,7},{6,0},{7,1},{8,10},{9,11},{10,... | collective-permute-start | bytes 1572872 | tf_op jit(solution)/shard_map/ppermute | solution.py:398
  167.3 19.2 %all-to-all-start.2 = ((bf16[32,32,128]{2,1,0:T(8,128)(2,1)}), bf16[32,32,128]{2,1,0:T(8,128)(2,1)S(1)}, u32[]{:S(2)}, u32[]{:S(2)}) async-start(bf16[32,32,128]{2,1,0:T(8,128)(2,1)} %pad_maximum_fusion.2), calls=%async_computation.2 | async-start | bytes 524288 | tf_op jit(solution)/shard_map/all_to_all | solution.py:390
  186.5 20.7 %all-to-all-start.3 = ((bf16[32,64,128]{2,1,0:T(8,128)(2,1)}), bf16[32,64,128]{2,1,0:T(8,128)(2,1)S(1)}, u32[]{:S(2)}, u32[]{:S(2)}) async-start(bf16[32,64,128]{2,1,0:T(8,128)(2,1)} %add_convert_fusion), calls=%async_computation.3 | async-start | bytes 1048576 | tf_op jit(solution)/shard_map/all_to_all | solution.py:390
  (17 other events, 180.5 us)

commit v3 on v1

--- a/solution.py
+++ b/solution.py
@@ -312,6 +312,14 @@
     key_column = lax.broadcasted_iota(jnp.int32, (ROWS, DH), 1)
     ones = jnp.where(key_column < 3, 1.0, 0.0).astype(bf16)
 
+    out_copies = [
+        pltpu.make_async_copy(kv_grad.at[pl.ds(i * MEMBERS, MEMBERS)], out, out_sems.at[k])
+        for k, (i, out) in enumerate(
+            [(0, outs[0]), (1, outs[1]), (2, outs[2].at[0]), (4, outs[2].at[1])]
+            + [(3, outs[3].at[0]), (5, outs[3].at[1]), (6, outs[4]), (7, outs[5])]
+        )
+    ]
+
     def backward(i, _):
         group = meta_ref[16 + i]
 
@@ -335,18 +343,11 @@
             kv_grad[members, :, :] = jnp.zeros((MEMBERS, 2 * SHARD, DH), bf16)
 
         by_visibility(meta_ref, group, compute, skip)
+        for k, block in enumerate((0, 1, 2, 4, 3, 5, 6, 7)):
+            pl.when(i == block)(out_copies[k].start)
         return 0
 
     lax.fori_loop(0, 8, backward, 0)
-    out_copies = [
-        pltpu.make_async_copy(kv_grad.at[pl.ds(i * MEMBERS, MEMBERS)], out, out_sems.at[k])
-        for k, (i, out) in enumerate(
-            [(0, outs[0]), (1, outs[1]), (2, outs[2].at[0]), (4, outs[2].at[1])]
-            + [(3, outs[3].at[0]), (5, outs[3].at[1]), (6, outs[4]), (7, outs[5])]
-        )
-    ]
-    for copy in out_copies:
-        copy.start()
     query_grad = (dqt[...] * scale).T.astype(bf16)
     own_first = meta_ref[10] > 0
     first, second = query_grad[:HALF], query_grad[HALF:]

time: 205 us -> 204 us (level)
  transfers between devices with their start and end apart: 33 -> 33, of which waited for: 15 -> 13; matrix products, arithmetic and copies ran while one was open for 3% -> 3% of each run, Pallas kernels for 10% -> 10%
where the time goes in v3:
time: 204 us
  waiting for transfers between devices  53.8 us (26%)
  Pallas kernels  52.2 us (26%)
  starting transfers between devices  45.3 us (22%)
  blocking collectives  43.5 us (21%)
  local copies, waits for them, and re-layouts  4.09 us (2%)
  other arithmetic  3.95 us (2%)
    all_to_all x1, blocking collectives, exchange(): lax.all_to_all(packed, 'seq', split_axis=0, concat_axis=0, tiled=True)  43.5 us
    pallas_call x1, Pallas kernels, student(): pl.pallas_call(student_kernel, out_shape=[half, half, one, one, two, two,...  27.9 us
    ppermute x14, waiting for transfers between devices, chip_shift(): lax.ppermute(x, 'blk', [(i, (i // 2 + by) % 4 * 2 + i % 2) for i in range...  26.9 us
    all_to_all x3, waiting for transfers between devices, exchange(): lax.all_to_all(packed, 'seq', split_axis=0, concat_axis=0, tiled=True)  21.4 us
    all_to_all x3, starting transfers between devices, exchange(): lax.all_to_all(packed, 'seq', split_axis=0, concat_axis=0, tiled=True)  19.1 us
    ppermute x14, starting transfers between devices, chip_shift(): lax.ppermute(x, 'blk', [(i, (i // 2 + by) % 4 * 2 + i % 2) for i in range...  16.4 us
    pallas_call x1, Pallas kernels, teacher(): pl.pallas_call(functools.partial(teacher_kernel, len(state), len(pieces),...  16.3 us
    ppermute x14, starting transfers between devices, swap_cores(): return lax.ppermute(x, 'blk', [(i, i ^ 1) for i in range(8)])  9.77 us
  transfers between devices with their start and end apart: 33, of which 13 were waited for; matrix products, arithmetic and copies ran while one was open for 3% of the time, Pallas kernels for 10%

profile of v3, /device:TPU:32, one launch (start us, length us, event | category | flops | bytes accessed | tf_op | source)
XLA Modules:
  0.0 203.9 jit_solution(2157418370894347067)
XLA Ops:
  0.6 2.5 %shard_map.94 = bf16[32,144,128]{2,1,0:T(8,128)(2,1)} custom-call(bf16[32,4096]{1,0:T(8,128)(2,1)} %bitcast.38, bf16[32,4096]{1,0:T(8,128)(2,1)} %bitcast.39, bf16[32,4096]{1,0:T(8,128)(2,1)} %bitcast.40, bf16[32,4096]{1,0:T(8,128)(2,1)} %bitcast.41, s32[1,32]{1,0:T(1,128)} %refs_4_.1), custom_call_target="tpu_custom_call" | custom-call | tf_op jit(solution)/shard_map/pallas_call | solution.py:56
  3.1 43.5 %all_to_all.20 = bf16[32,144,128]{2,1,0:T(8,128)(2,1)S(1)} all-to-all(bf16[32,144,128]{2,1,0:T(8,128)(2,1)} %shard_map.94), channel_id=1, replica_groups=mesh['seq'=32,'blk'=8] {'seq'}, dimensions={0} | all-to-all | bytes 2359296 | tf_op jit(solution)/shard_map/all_to_all | solution.py:391
  46.7 1.6 collective-permute-start.9
  48.3 1.7 collective-permute-start.7
  50.0 1.9 shard_map.95
  52.0 4.6 %all-to-all-start.1 = ((bf16[32,64,128]{2,1,0:T(8,128)(2,1)}), bf16[32,64,128]{2,1,0:T(8,128)(2,1)S(1)}, u32[]{:S(2)}, u32[]{:S(2)}) async-start(bf16[32,64,128]{2,1,0:T(8,128)(2,1)} %shard_map.95), calls=%async_computation.1 | async-start | bytes 1048576 | tf_op jit(solution)/shard_map/all_to_all | solution.py:391
  57.4 1.7 collective-permute-start
  62.1 4.2 %collective-permute-done.1 = f32[8,128]{0,1:T(8,128)S(1)} collective-permute-done((f32[8,128]{0,1:T(8,128)S(1)}, f32[8,128]{0,1:T(8,128)S(1)}, u32[]{:S(2)}, u32[]{:S(2)}) %collective-permute-start.1) | collective-permute-done | bytes 4128 | tf_op jit(solution)/shard_map/ppermute | solution.py:399
  67.2 1.6 collective-permute-start.8
  68.8 3.2 %collective-permute-done.11.rest_6_ = bf16[16,64,128]{2,1,0:T(8,128)(2,1)S(1)} collective-permute-done((bf16[16,64,128]{2,1,0:T(8,128)(2,1)S(1)}, bf16[16,64,128]{2,1,0:T(8,128)(2,1)S(1)}, u32[]{:S(2)}, u32[]{:S(2)}) %collective-permute-start.11) | collective-permute-done | bytes 262176 | tf_op jit(solution)/shard_map/ppermute | solution.py:399
  71.9 1.2 collective-permute-start.13
  74.1 1.3 collective-permute-start.14
  77.3 1.5 collective-permute-start.5
  79.4 16.3 %shard_map.96.target_ref = bf16[128,1024]{1,0:T(8,128)(2,1)} custom-call(s32[24]{0:T(128)} %concatenate.20.meta_ref, bf16[16,64,128]{2,1,0:T(8,128)(2,1)} %get-tuple-element.46.own_ref, bf16[16,64,128]{2,1,0:T(8,128)(2,1)} %copy-done.13, bf16[32,64,128]{2,1,0:T(8,128)(2,1)} %copy-done.5, bf16[32,64,128]{2,1,0:T(8,128)(2,1)} %copy-done.10, ...), custom_call_target="tpu_custom_call" | custom-call | flops 15360000000 | bytes 4194304 | tf_op jit(solution)/shard_map/pallas_call | solution.py:210
  95.8 2.7 %collective-permute-start.19 = (bf16[16,64,128]{2,1,0:T(8,128)(2,1)S(1)}, bf16[16,64,128]{2,1,0:T(8,128)(2,1)S(1)}, u32[]{:S(2)}, u32[]{:S(2)}) collective-permute-start(bf16[16,64,128]{2,1,0:T(8,128)(2,1)S(1)} %slice.53), channel_id=1, source_target_pairs={{0,6},{1,7},{2,0},{3,1},{4,2},{5,3},{6,4},{7,5},{8,14},{9,15},{10,... | collective-permute-start | bytes 786440 | tf_op jit(solution)/shard_map/ppermute | solution.py:399
  99.1 5.1 %collective-permute-done.19.rest_7_ = bf16[16,64,128]{2,1,0:T(8,128)(2,1)S(1)} collective-permute-done((bf16[16,64,128]{2,1,0:T(8,128)(2,1)S(1)}, bf16[16,64,128]{2,1,0:T(8,128)(2,1)S(1)}, u32[]{:S(2)}, u32[]{:S(2)}) %collective-permute-start.19) | collective-permute-done | bytes 262176 | tf_op jit(solution)/shard_map/ppermute | solution.py:399
  104.1 4.3 %collective-permute-done.18.rest_6_ = bf16[16,64,128]{2,1,0:T(8,128)(2,1)S(1)} collective-permute-done((bf16[16,64,128]{2,1,0:T(8,128)(2,1)S(1)}, bf16[16,64,128]{2,1,0:T(8,128)(2,1)S(1)}, u32[]{:S(2)}, u32[]{:S(2)}) %collective-permute-start.18) | collective-permute-done | bytes 262176 | tf_op jit(solution)/shard_map/ppermute | solution.py:399
  110.2 27.9 %shard_map.97 = (bf16[16,32,128]{2,1,0:T(8,128)(2,1)}, bf16[16,32,128]{2,1,0:T(8,128)(2,1)}, bf16[32,64,128]{2,1,0:T(8,128)(2,1)}, bf16[32,64,128]{2,1,0:T(8,128...) custom-call(s32[24]{0:T(128)} %concatenate.19.meta_ref, ...), custom_call_target="tpu_custom_call" | custom-call | flops 25999998976 | bytes 10485760 | tf_op jit(solution)/shard_map/pallas_call | solution.py:365
  138.1 2.4 %collective-permute-start.24 = (bf16[2,32,64,128]{3,2,1,0:T(8,128)(2,1)}, bf16[2,32,64,128]{3,2,1,0:T(8,128)(2,1)S(1)}, u32[]{:S(2)}, u32[]{:S(2)}) collective-permute-start(bf16[2,32,64,128]{3,2,1,0:T(8,128)(2,1)} %get-tuple-element.30), channel_id=1, source_target_pairs={{0,1},{1,0},{2,3},{3,2},{4,5},{5,4},{6,7},{7,6},{8,9},{9,8},{10,11... | collective-permute-start | bytes 3145736 | tf_op jit(solution)/shard_map/ppermute | solution.py:403
  141.0 2.7 %collective-permute-done.25 = bf16[32,64,128]{2,1,0:T(8,128)(2,1)S(1)} collective-permute-done((bf16[32,64,128]{2,1,0:T(8,128)(2,1)}, bf16[32,64,128]{2,1,0:T(8,128)(2,1)S(1)}, u32[]{:S(2)}, u32[]{:S(2)}) %collective-permute-start.25) | collective-permute-done | bytes 524320 | tf_op jit(solution)/shard_map/ppermute | solution.py:403
  143.7 1.2 add_convert_fusion.1
  145.6 2.7 %collective-permute-start.28 = (bf16[16,64,128]{2,1,0:T(8,128)(2,1)S(1)}, bf16[16,64,128]{2,1,0:T(8,128)(2,1)S(1)}, u32[]{:S(2)}, u32[]{:S(2)}) collective-permute-start(bf16[16,64,128]{2,1,0:T(8,128)(2,1)S(1)} %get-tuple-element.44), channel_id=1, source_target_pairs={{0,6},{1,7},{2,0},{3,1},{4,2},{5,3},{6,4},{7,5},{8,14},{9,15},{10,... | collective-permute-start | bytes 786440 | tf_op jit(solution)/shard_map/ppermute | solution.py:399
  148.9 6.0 %collective-permute-done.26 = bf16[16,64,128]{2,1,0:T(8,128)(2,1)S(1)} collective-permute-done((bf16[16,64,128]{2,1,0:T(8,128)(2,1)S(1)}, bf16[16,64,128]{2,1,0:T(8,128)(2,1)S(1)}, u32[]{:S(2)}, u32[]{:S(2)}) %collective-permute-start.26) | collective-permute-done | bytes 262176 | tf_op jit(solution)/shard_map/ppermute | solution.py:399
  155.1 3.0 %collective-permute-start.29 = (bf16[32,64,128]{2,1,0:T(8,128)(2,1)S(1)}, bf16[32,64,128]{2,1,0:T(8,128)(2,1)S(1)}, u32[]{:S(2)}, u32[]{:S(2)}) collective-permute-start(bf16[32,64,128]{2,1,0:T(8,128)(2,1)S(1)} %pad_maximum_fusion.1), channel_id=1, source_target_pairs={{0,6},{1,7},{2,0},{3,1},{4,2},{5,3},{6,4},{7,5},{8,14},{9,15},{10,... | collective-permute-start | bytes 1572872 | tf_op jit(solution)/shard_map/ppermute | solution.py:399
  159.1 9.9 %all-to-all-start.2 = ((bf16[32,32,128]{2,1,0:T(8,128)(2,1)}), bf16[32,32,128]{2,1,0:T(8,128)(2,1)S(1)}, u32[]{:S(2)}, u32[]{:S(2)}) async-start(bf16[32,32,128]{2,1,0:T(8,128)(2,1)} %pad_maximum_fusion.2), calls=%async_computation.2 | async-start | bytes 524288 | tf_op jit(solution)/shard_map/all_to_all | solution.py:391
  169.0 3.3 %collective-permute-done.27 = bf16[32,64,128]{2,1,0:T(8,128)(2,1)S(1)} collective-permute-done((bf16[32,64,128]{2,1,0:T(8,128)(2,1)S(1)}, bf16[32,64,128]{2,1,0:T(8,128)(2,1)S(1)}, u32[]{:S(2)}, u32[]{:S(2)}) %collective-permute-start.27) | collective-permute-done | bytes 524320 | tf_op jit(solution)/shard_map/ppermute | solution.py:399
  172.3 1.2 add_convert_fusion
  173.5 6.9 %all-to-all-done.2.in_ref = bf16[32,32,128]{2,1,0:T(8,128)(2,1)S(1)} async-done(((bf16[32,32,128]{2,1,0:T(8,128)(2,1)}), bf16[32,32,128]{2,1,0:T(8,128)(2,1)S(1)}, u32[]{:S(2)}, u32[]{:S(2)}) %all-to-all-start.2) | async-done | bytes 262176 | tf_op jit(solution)/shard_map/all_to_all | solution.py:391
  180.4 4.6 %all-to-all-start.3 = ((bf16[32,64,128]{2,1,0:T(8,128)(2,1)}), bf16[32,64,128]{2,1,0:T(8,128)(2,1)S(1)}, u32[]{:S(2)}, u32[]{:S(2)}) async-start(bf16[32,64,128]{2,1,0:T(8,128)(2,1)} %add_convert_fusion), calls=%async_computation.3 | async-start | bytes 1048576 | tf_op jit(solution)/shard_map/all_to_all | solution.py:391
  185.0 1.7 shard_map.98
  186.7 14.4 %all-to-all-done.3.in_ref = bf16[32,64,128]{2,1,0:T(8,128)(2,1)S(1)} async-done(((bf16[32,64,128]{2,1,0:T(8,128)(2,1)}), bf16[32,64,128]{2,1,0:T(8,128)(2,1)S(1)}, u32[]{:S(2)}, u32[]{:S(2)}) %all-to-all-start.3) | async-done | bytes 524320 | tf_op jit(solution)/shard_map/all_to_all | solution.py:391
  201.9 1.9 shard_map.99
  (102 shorter events, 13.9 us)
Async XLA Ops:
  46.7 13.9 %collective-permute-start.9 = (bf16[32,64,128]{2,1,0:T(8,128)(2,1)S(1)}, bf16[32,64,128]{2,1,0:T(8,128)(2,1)S(1)}, u32[]{:S(2)}, u32[]{:S(2)}) collective-permute-start(bf16[32,64,128]{2,1,0:T(8,128)(2,1)S(1)} %get-tuple-element.39.rest_0_), channel_id=1, source_target_pairs={{0,2},{1,3},{2,4},{3,5},{4,6},{5,7},{6,0},{7,1},{8,10},{9,11},{10,... | collective-permute-start | bytes 1572872 | tf_op jit(solution)/shard_map/ppermute | solution.py:399
  48.3 12.8 %collective-permute-start.7 = (bf16[32,64,128]{2,1,0:T(8,128)(2,1)S(1)}, bf16[32,64,128]{2,1,0:T(8,128)(2,1)}, u32[]{:S(2)}, u32[]{:S(2)}) collective-permute-start(bf16[32,64,128]{2,1,0:T(8,128)(2,1)S(1)} %get-tuple-element.39.rest_0_), channel_id=1, source_target_pairs={{0,6},{1,7},{2,0},{3,1},{4,2},{5,3},{6,4},{7,5},{8,14},{9,15},{10,... | collective-permute-start | bytes 1572872 | tf_op jit(solution)/shard_map/ppermute | solution.py:399
  52.0 25.2 %all-to-all-start.1 = ((bf16[32,64,128]{2,1,0:T(8,128)(2,1)}), bf16[32,64,128]{2,1,0:T(8,128)(2,1)S(1)}, u32[]{:S(2)}, u32[]{:S(2)}) async-start(bf16[32,64,128]{2,1,0:T(8,128)(2,1)} %shard_map.95), calls=%async_computation.1 | async-start | bytes 1048576 | tf_op jit(solution)/shard_map/all_to_all | solution.py:391
  57.3 9.8 %collective-permute-start.3 = (bf16[16,64,128]{2,1,0:T(8,128)(2,1)S(1)}, bf16[16,64,128]{2,1,0:T(8,128)(2,1)S(1)}, u32[]{:S(2)}, u32[]{:S(2)}) collective-permute-start(bf16[16,64,128]{2,1,0:T(8,128)(2,1)S(1)} %get-tuple-element.45), channel_id=1, source_target_pairs={{0,7},{1,6},{2,5},{3,4},{4,3},{5,2},{6,1},{7,0},{8,15},{9,14},{10,... | collective-permute-start | bytes 786440 | tf_op jit(solution)/shard_map/ppermute | solution.py:395
  57.4 2.6 %collective-permute-start = (f32[8,128]{0,1:T(8,128)S(1)}, f32[8,128]{0,1:T(8,128)S(1)}, u32[]{:S(2)}, u32[]{:S(2)}) collective-permute-start(f32[8,128]{0,1:T(8,128)S(1)} %broadcast_in_dim.21), channel_id=1, source_target_pairs={{0,1},{1,0},{2,3},{3,2},{4,5},{5,4},{6,7},{7,6},{8,9},{9,8},{10,11... | collective-permute-start | bytes 12296 | tf_op jit(solution)/shard_map/ppermute | solution.py:403
  60.1 6.3 %collective-permute-start.1 = (f32[8,128]{0,1:T(8,128)S(1)}, f32[8,128]{0,1:T(8,128)S(1)}, u32[]{:S(2)}, u32[]{:S(2)}) collective-permute-start(f32[8,128]{0,1:T(8,128)S(1)} %broadcast_add_fusion), channel_id=1, source_target_pairs={{0,2},{1,3},{2,4},{3,5},{4,6},{5,7},{6,0},{7,1},{8,10},{9,11},{10,... | collective-permute-start | bytes 12296 | tf_op jit(solution)/shard_map/ppermute | solution.py:399
  60.3 15.7 %collective-permute-start.6 = (bf16[32,64,128]{2,1,0:T(8,128)(2,1)S(1)}, bf16[32,64,128]{2,1,0:T(8,128)(2,1)S(1)}, u32[]{:S(2)}, u32[]{:S(2)}) collective-permute-start(bf16[32,64,128]{2,1,0:T(8,128)(2,1)S(1)} %get-tuple-element.39.rest_0_), channel_id=1, source_target_pairs={{0,1},{1,0},{2,3},{3,2},{4,5},{5,4},{6,7},{7,6},{8,9},{9,8},{10,11... | collective-permute-start | bytes 1572872 | tf_op jit(solution)/shard_map/ppermute | solution.py:403
  60.6 11.3 %collective-permute-start.11 = (bf16[16,64,128]{2,1,0:T(8,128)(2,1)S(1)}, bf16[16,64,128]{2,1,0:T(8,128)(2,1)S(1)}, u32[]{:S(2)}, u32[]{:S(2)}) collective-permute-start(bf16[16,64,128]{2,1,0:T(8,128)(2,1)S(1)} %slice.62), channel_id=1, source_target_pairs={{0,2},{1,3},{2,4},{3,5},{4,6},{5,7},{6,0},{7,1},{8,10},{9,11},{10,... | collective-permute-start | bytes 786440 | tf_op jit(solution)/shard_map/ppermute | solution.py:399
  61.1 16.2 %collective-permute-start.10 = (bf16[32,64,128]{2,1,0:T(8,128)(2,1)S(1)}, bf16[32,64,128]{2,1,0:T(8,128)(2,1)}, u32[]{:S(2)}, u32[]{:S(2)}) collective-permute-start(bf16[32,64,128]{2,1,0:T(8,128)(2,1)S(1)} %collective-permute-done.9.rest_4_), channel_id=1, source_target_pairs={{0,1},{1,0},{2,3},{3,2},{4,5},{5,4},{6,7},{7,6},{8,9},{9,8},{10,11... | collective-permute-start | bytes 1572872 | tf_op jit(solution)/shard_map/ppermute | solution.py:403
  66.3 7.7 %collective-permute-start.12 = (bf16[16,64,128]{2,1,0:T(8,128)(2,1)S(1)}, bf16[16,64,128]{2,1,0:T(8,128)(2,1)S(1)}, u32[]{:S(2)}, u32[]{:S(2)}) collective-permute-start(bf16[16,64,128]{2,1,0:T(8,128)(2,1)S(1)} %slice.63), channel_id=1, source_target_pairs={{0,6},{1,7},{2,0},{3,1},{4,2},{5,3},{6,4},{7,5},{8,14},{9,15},{10,... | collective-permute-start | bytes 786440 | tf_op jit(solution)/shard_map/ppermute | solution.py:399
  67.2 12.2 %collective-permute-start.8 = (bf16[32,64,128]{2,1,0:T(8,128)(2,1)}, bf16[32,64,128]{2,1,0:T(8,128)(2,1)}, u32[]{:S(2)}, u32[]{:S(2)}) collective-permute-start(bf16[32,64,128]{2,1,0:T(8,128)(2,1)} %collective-permute-done.7.rest_2_), channel_id=1, source_target_pairs={{0,1},{1,0},{2,3},{3,2},{4,5},{5,4},{6,7},{7,6},{8,9},{9,8},{10,11... | collective-permute-start | bytes 1572872 | tf_op jit(solution)/shard_map/ppermute | solution.py:403
  71.9 5.2 %collective-permute-start.13 = (bf16[16,64,128]{2,1,0:T(8,128)(2,1)S(1)}, bf16[16,64,128]{2,1,0:T(8,128)(2,1)}, u32[]{:S(2)}, u32[]{:S(2)}) collective-permute-start(bf16[16,64,128]{2,1,0:T(8,128)(2,1)S(1)} %collective-permute-done.11.rest_6_), channel_id=1, source_target_pairs={{0,1},{1,0},{2,3},{3,2},{4,5},{5,4},{6,7},{7,6},{8,9},{9,8},{10,11... | collective-permute-start | bytes 786440 | tf_op jit(solution)/shard_map/ppermute | solution.py:403
  74.1 4.7 %collective-permute-start.14 = (bf16[16,64,128]{2,1,0:T(8,128)(2,1)S(1)}, bf16[16,64,128]{2,1,0:T(8,128)(2,1)}, u32[]{:S(2)}, u32[]{:S(2)}) collective-permute-start(bf16[16,64,128]{2,1,0:T(8,128)(2,1)S(1)} %collective-permute-done.12.rest_7_), channel_id=1, source_target_pairs={{0,1},{1,0},{2,3},{3,2},{4,5},{5,4},{6,7},{7,6},{8,9},{9,8},{10,11... | collective-permute-start | bytes 786440 | tf_op jit(solution)/shard_map/ppermute | solution.py:403
  76.0 23.1 %collective-permute-start.2 = (f32[8,128]{0,1:T(8,128)S(1)}, f32[8,128]{0,1:T(8,128)S(1)}, u32[]{:S(2)}, u32[]{:S(2)}) collective-permute-start(f32[8,128]{0,1:T(8,128)S(1)} %fusion.9), channel_id=1, source_target_pairs={{0,4},{1,5},{2,6},{3,7},{4,0},{5,1},{6,2},{7,3},{8,12},{9,13},{10,... | collective-permute-start | bytes 12296 | tf_op jit(solution)/shard_map/ppermute | solution.py:399
  77.1 32.0 %collective-permute-start.15 = (bf16[32,64,128]{2,1,0:T(8,128)(2,1)S(1)}, bf16[32,64,128]{2,1,0:T(8,128)(2,1)}, u32[]{:S(2)}, u32[]{:S(2)}) collective-permute-start(bf16[32,64,128]{2,1,0:T(8,128)(2,1)S(1)} %all-to-all-done.1.rest_0_), channel_id=1, source_target_pairs={{0,1},{1,0},{2,3},{3,2},{4,5},{5,4},{6,7},{7,6},{8,9},{9,8},{10,11... | collective-permute-start | bytes 1572872 | tf_op jit(solution)/shard_map/ppermute | solution.py:403
  77.3 18.5 %collective-permute-start.5 = (bf16[32,64,128]{2,1,0:T(8,128)(2,1)S(1)}, bf16[32,64,128]{2,1,0:T(8,128)(2,1)S(1)}, u32[]{:S(2)}, u32[]{:S(2)}) collective-permute-start(bf16[32,64,128]{2,1,0:T(8,128)(2,1)S(1)} %all-to-all-done.1.rest_0_), channel_id=1, source_target_pairs={{0,6},{1,7},{2,0},{3,1},{4,2},{5,3},{6,4},{7,5},{8,14},{9,15},{10,... | collective-permute-start | bytes 1572872 | tf_op jit(solution)/shard_map/ppermute | solution.py:399
  78.8 17.0 %collective-permute-start.4 = (bf16[32,64,128]{2,1,0:T(8,128)(2,1)S(1)}, bf16[32,64,128]{2,1,0:T(8,128)(2,1)S(1)}, u32[]{:S(2)}, u32[]{:S(2)}) collective-permute-start(bf16[32,64,128]{2,1,0:T(8,128)(2,1)S(1)} %all-to-all-done.1.rest_0_), channel_id=1, source_target_pairs={{0,2},{1,3},{2,4},{3,5},{4,6},{5,7},{6,0},{7,1},{8,10},{9,11},{10,... | collective-permute-start | bytes 1572872 | tf_op jit(solution)/shard_map/ppermute | solution.py:399
  95.8 8.3 %collective-permute-start.19 = (bf16[16,64,128]{2,1,0:T(8,128)(2,1)S(1)}, bf16[16,64,128]{2,1,0:T(8,128)(2,1)S(1)}, u32[]{:S(2)}, u32[]{:S(2)}) collective-permute-start(bf16[16,64,128]{2,1,0:T(8,128)(2,1)S(1)} %slice.53), channel_id=1, source_target_pairs={{0,6},{1,7},{2,0},{3,1},{4,2},{5,3},{6,4},{7,5},{8,14},{9,15},{10,... | collective-permute-start | bytes 786440 | tf_op jit(solution)/shard_map/ppermute | solution.py:399
  98.5 10.6 %collective-permute-start.16 = (bf16[32,64,128]{2,1,0:T(8,128)(2,1)S(1)}, bf16[32,64,128]{2,1,0:T(8,128)(2,1)S(1)}, u32[]{:S(2)}, u32[]{:S(2)}) collective-permute-start(bf16[32,64,128]{2,1,0:T(8,128)(2,1)S(1)} %collective-permute-done.5.rest_2_), channel_id=1, source_target_pairs={{0,1},{1,0},{2,3},{3,2},{4,5},{5,4},{6,7},{7,6},{8,9},{9,8},{10,11... | collective-permute-start | bytes 1572872 | tf_op jit(solution)/shard_map/ppermute | solution.py:403
  98.5 10.6 %collective-permute-start.17 = (bf16[32,64,128]{2,1,0:T(8,128)(2,1)S(1)}, bf16[32,64,128]{2,1,0:T(8,128)(2,1)S(1)}, u32[]{:S(2)}, u32[]{:S(2)}) collective-permute-start(bf16[32,64,128]{2,1,0:T(8,128)(2,1)S(1)} %collective-permute-done.4.rest_4_), channel_id=1, source_target_pairs={{0,1},{1,0},{2,3},{3,2},{4,5},{5,4},{6,7},{7,6},{8,9},{9,8},{10,11... | collective-permute-start | bytes 1572872 | tf_op jit(solution)/shard_map/ppermute | solution.py:403
  99.1 9.4 %collective-permute-start.18 = (bf16[16,64,128]{2,1,0:T(8,128)(2,1)S(1)}, bf16[16,64,128]{2,1,0:T(8,128)(2,1)S(1)}, u32[]{:S(2)}, u32[]{:S(2)}) collective-permute-start(bf16[16,64,128]{2,1,0:T(8,128)(2,1)S(1)} %slice.52), channel_id=1, source_target_pairs={{0,2},{1,3},{2,4},{3,5},{4,6},{5,7},{6,0},{7,1},{8,10},{9,11},{10,... | collective-permute-start | bytes 786440 | tf_op jit(solution)/shard_map/ppermute | solution.py:399
  104.1 5.0 %collective-permute-start.21 = (bf16[16,64,128]{2,1,0:T(8,128)(2,1)S(1)}, bf16[16,64,128]{2,1,0:T(8,128)(2,1)}, u32[]{:S(2)}, u32[]{:S(2)}) collective-permute-start(bf16[16,64,128]{2,1,0:T(8,128)(2,1)S(1)} %collective-permute-done.19.rest_7_), channel_id=1, source_target_pairs={{0,1},{1,0},{2,3},{3,2},{4,5},{5,4},{6,7},{7,6},{8,9},{9,8},{10,11... | collective-permute-start | bytes 786440 | tf_op jit(solution)/shard_map/ppermute | solution.py:403
  138.1 10.3 %collective-permute-start.24 = (bf16[2,32,64,128]{3,2,1,0:T(8,128)(2,1)}, bf16[2,32,64,128]{3,2,1,0:T(8,128)(2,1)S(1)}, u32[]{:S(2)}, u32[]{:S(2)}) collective-permute-start(bf16[2,32,64,128]{3,2,1,0:T(8,128)(2,1)} %get-tuple-element.30), channel_id=1, source_target_pairs={{0,1},{1,0},{2,3},{3,2},{4,5},{5,4},{6,7},{7,6},{8,9},{9,8},{10,11... | collective-permute-start | bytes 3145736 | tf_op jit(solution)/shard_map/ppermute | solution.py:403
  140.5 3.2 %collective-permute-start.25 = (bf16[32,64,128]{2,1,0:T(8,128)(2,1)}, bf16[32,64,128]{2,1,0:T(8,128)(2,1)S(1)}, u32[]{:S(2)}, u32[]{:S(2)}) collective-permute-start(bf16[32,64,128]{2,1,0:T(8,128)(2,1)} %get-tuple-element.32), channel_id=1, source_target_pairs={{0,1},{1,0},{2,3},{3,2},{4,5},{5,4},{6,7},{7,6},{8,9},{9,8},{10,11... | collective-permute-start | bytes 1572872 | tf_op jit(solution)/shard_map/ppermute | solution.py:403
  140.6 17.7 %collective-permute-start.22 = (bf16[16,32,128]{2,1,0:T(8,128)(2,1)}, bf16[16,32,128]{2,1,0:T(8,128)(2,1)S(1)}, u32[]{:S(2)}, u32[]{:S(2)}) collective-permute-start(bf16[16,32,128]{2,1,0:T(8,128)(2,1)} %get-tuple-element.26), channel_id=1, source_target_pairs={{0,7},{1,6},{2,5},{3,4},{4,3},{5,2},{6,1},{7,0},{8,15},{9,14},{10,... | collective-permute-start | bytes 393224 | tf_op jit(solution)/shard_map/ppermute | solution.py:395
  140.6 28.4 %collective-permute-start.23 = (bf16[32,64,128]{2,1,0:T(8,128)(2,1)}, bf16[32,64,128]{2,1,0:T(8,128)(2,1)S(1)}, u32[]{:S(2)}, u32[]{:S(2)}) collective-permute-start(bf16[32,64,128]{2,1,0:T(8,128)(2,1)} %get-tuple-element.28), channel_id=1, source_target_pairs={{0,1},{1,0},{2,3},{3,2},{4,5},{5,4},{6,7},{7,6},{8,9},{9,8},{10,11... | collective-permute-start | bytes 1572872 | tf_op jit(solution)/shard_map/ppermute | solution.py:403
  145.0 9.9 %collective-permute-start.26 = (bf16[16,64,128]{2,1,0:T(8,128)(2,1)S(1)}, bf16[16,64,128]{2,1,0:T(8,128)(2,1)S(1)}, u32[]{:S(2)}, u32[]{:S(2)}) collective-permute-start(bf16[16,64,128]{2,1,0:T(8,128)(2,1)S(1)} %get-tuple-element.43), channel_id=1, source_target_pairs={{0,2},{1,3},{2,4},{3,5},{4,6},{5,7},{6,0},{7,1},{8,10},{9,11},{10,... | collective-permute-start | bytes 786440 | tf_op jit(solution)/shard_map/ppermute | solution.py:399
  145.6 9.3 %collective-permute-start.28 = (bf16[16,64,128]{2,1,0:T(8,128)(2,1)S(1)}, bf16[16,64,128]{2,1,0:T(8,128)(2,1)S(1)}, u32[]{:S(2)}, u32[]{:S(2)}) collective-permute-start(bf16[16,64,128]{2,1,0:T(8,128)(2,1)S(1)} %get-tuple-element.44), channel_id=1, source_target_pairs={{0,6},{1,7},{2,0},{3,1},{4,2},{5,3},{6,4},{7,5},{8,14},{9,15},{10,... | collective-permute-start | bytes 786440 | tf_op jit(solution)/shard_map/ppermute | solution.py:399
  155.1 13.9 %collective-permute-start.29 = (bf16[32,64,128]{2,1,0:T(8,128)(2,1)S(1)}, bf16[32,64,128]{2,1,0:T(8,128)(2,1)S(1)}, u32[]{:S(2)}, u32[]{:S(2)}) collective-permute-start(bf16[32,64,128]{2,1,0:T(8,128)(2,1)S(1)} %pad_maximum_fusion.1), channel_id=1, source_target_pairs={{0,6},{1,7},{2,0},{3,1},{4,2},{5,3},{6,4},{7,5},{8,14},{9,15},{10,... | collective-permute-start | bytes 1572872 | tf_op jit(solution)/shard_map/ppermute | solution.py:399
  158.2 14.1 %collective-permute-start.27 = (bf16[32,64,128]{2,1,0:T(8,128)(2,1)S(1)}, bf16[32,64,128]{2,1,0:T(8,128)(2,1)S(1)}, u32[]{:S(2)}, u32[]{:S(2)}) collective-permute-start(bf16[32,64,128]{2,1,0:T(8,128)(2,1)S(1)} %pad_maximum_fusion), channel_id=1, source_target_pairs={{0,2},{1,3},{2,4},{3,5},{4,6},{5,7},{6,0},{7,1},{8,10},{9,11},{10,... | collective-permute-start | bytes 1572872 | tf_op jit(solution)/shard_map/ppermute | solution.py:399
  159.1 21.3 %all-to-all-start.2 = ((bf16[32,32,128]{2,1,0:T(8,128)(2,1)}), bf16[32,32,128]{2,1,0:T(8,128)(2,1)S(1)}, u32[]{:S(2)}, u32[]{:S(2)}) async-start(bf16[32,32,128]{2,1,0:T(8,128)(2,1)} %pad_maximum_fusion.2), calls=%async_computation.2 | async-start | bytes 524288 | tf_op jit(solution)/shard_map/all_to_all | solution.py:391
  180.4 20.7 %all-to-all-start.3 = ((bf16[32,64,128]{2,1,0:T(8,128)(2,1)}), bf16[32,64,128]{2,1,0:T(8,128)(2,1)S(1)}, u32[]{:S(2)}, u32[]{:S(2)}) async-start(bf16[32,64,128]{2,1,0:T(8,128)(2,1)} %add_convert_fusion), calls=%async_computation.3 | async-start | bytes 1048576 | tf_op jit(solution)/shard_map/all_to_all | solution.py:391
  (19 other events, 157.1 us)
